TPU v7x, 256 devices: a whole 4x4x8 slice. The times are simulated.
256 devices in a mesh: dp: 16 (over z, x_hi), expert: 16 (over y, x_lo, core).
Axes of the slice: x: 4 (x_hi: 2, x_lo: 2; x = x_hi * 2 + x_lo), y: 4, z: 8, core: 2. Of those that a mesh axis runs over, the one named last changes fastest.
Arguments:
- tokens: bfloat16 [65536, 1024], P(('dp', 'expert')), may hold values from -24 to 24
- expert_ids: int32 [65536, 2], P(('dp', 'expert')), may hold values from 0 to 31, all different within a row; in each aligned block of 256 rows (0 to 255, 256 to 511, ...) at most 40 rows name the same one
- gate_quant: int32 [65536], P(('dp', 'expert')), may hold values from 1 to 255
- cotangent: bfloat16 [65536, 1024], P(('dp', 'expert')), may hold values from -3 to 3
- w_gate: bfloat16 [32, 1024, 512], P('expert'), may hold values from -0.1875 to 0.1875
- w_up: bfloat16 [32, 1024, 512], P('expert'), may hold values from -0.1875 to 0.1875
- w_down: bfloat16 [32, 512, 1024], P('expert'), may hold values from -0.25 to 0.25
Outputs:
- layer_out: bfloat16 [65536, 1024], P(('dp', 'expert'))
- grad_tokens: bfloat16 [65536, 1024], P(('dp', 'expert'))
- grad_w_gate: float32 [32, 1024, 512], P('expert', 'dp')
- grad_w_up: float32 [32, 1024, 512], P('expert', 'dp')
- grad_w_down: float32 [32, 512, 1024], P('expert', 'dp')
Inputs may be any that keep to these rules, and one draw needn't show every extreme that they name: `expert_ids`: each row names two different experts. Within the 256 rows of one device no expert is named more than 40 times, and in every draw some device names some expert exactly 40 times.
All inputs are finite; a program needn't handle non-finite values.
Results may differ from a plain program's by a relative error of at most 0.017.
Values may be sent and summed in bfloat16 or wider, within the bound.
No kernel may reach another device: no remote copies, remote signals or barrier semaphores. Data moves between devices by JAX's collectives and lax.ppermute only.
A program may use at most 128 MiB of HBM per device.

v0:
```python
import jax
import jax.numpy as jnp
from jax import lax
from jax.sharding import PartitionSpec as P

D = 1024
EXPERTS = 32
CAP = 40


def slot_places(expert_ids):
    flat_ids = expert_ids.reshape(-1)
    choose = (flat_ids[:, None] == jnp.arange(EXPERTS, dtype=jnp.int32)[None, :]).astype(jnp.int32)
    earlier = jnp.cumsum(choose, axis=0) - choose
    return flat_ids * CAP + jnp.sum(earlier * choose, axis=1)


def expert_forward(received, w_gate, w_up, w_down):
    gate_value = jnp.einsum(
        "aserd,edh->aserh", received, w_gate, preferred_element_type=jnp.float32
    )
    up_value = jnp.einsum("aserd,edh->aserh", received, w_up, preferred_element_type=jnp.float32)
    sigmoid_gate = jax.nn.sigmoid(gate_value)
    hidden = (gate_value * sigmoid_gate * up_value).astype(jnp.bfloat16)
    expert_out = jnp.einsum(
        "aserh,ehd->aserd", hidden, w_down, preferred_element_type=jnp.float32
    ).astype(jnp.bfloat16)
    return (gate_value, up_value, hidden, expert_out)


def expert_backward(routed, gate_value, up_value, w_gate, w_up, w_down):
    hidden_grad = jnp.einsum("aserd,ehd->aserh", routed, w_down, preferred_element_type=jnp.float32)
    sigmoid_gate = jax.nn.sigmoid(gate_value)
    gate_grad = (
        hidden_grad * up_value * sigmoid_gate * (1.0 + gate_value * (1.0 - sigmoid_gate))
    ).astype(jnp.bfloat16)
    up_grad = (hidden_grad * (gate_value * sigmoid_gate)).astype(jnp.bfloat16)
    input_grad = (
        jnp.einsum("aserh,edh->aserd", gate_grad, w_gate, preferred_element_type=jnp.float32)
        + jnp.einsum("aserh,edh->aserd", up_grad, w_up, preferred_element_type=jnp.float32)
    ).astype(jnp.bfloat16)
    return (gate_grad, up_grad, input_grad)


def per_device(tokens, expert_ids, gate_quant, cotangent, w_gate, w_up, w_down):
    groups = lax.axis_size("expert")
    local_experts = w_gate.shape[0]
    slot_index = slot_places(expert_ids)
    first_share = gate_quant.astype(jnp.float32) / 256.0
    shares = jnp.stack([first_share, 1.0 - first_share], axis=1)
    doubled = jnp.repeat(tokens, 2, axis=0)
    routed_rows = (
        (shares[:, :, None] * cotangent[:, None, :].astype(jnp.float32))
        .astype(jnp.bfloat16)
        .reshape(-1, D)
    )
    blank_rows = jnp.zeros((EXPERTS * CAP, D), jnp.bfloat16)
    layout = (groups, 1, local_experts, CAP, D)
    send_tokens = blank_rows.at[slot_index].set(doubled).reshape(layout)
    send_grads = blank_rows.at[slot_index].set(routed_rows).reshape(layout)
    received = lax.all_to_all(send_tokens, "expert", split_axis=0, concat_axis=1, tiled=True)
    gate_value, up_value, hidden, expert_out = expert_forward(received, w_gate, w_up, w_down)
    returned = lax.all_to_all(expert_out, "expert", split_axis=1, concat_axis=0, tiled=True)
    returned, received, gate_value, up_value, hidden = (
        returned,
        received,
        gate_value,
        up_value,
        hidden,
    )
    routed = lax.all_to_all(send_grads, "expert", split_axis=0, concat_axis=1, tiled=True)
    gate_grad, up_grad, input_grad = expert_backward(
        routed, gate_value, up_value, w_gate, w_up, w_down
    )
    returned_grad = lax.all_to_all(input_grad, "expert", split_axis=1, concat_axis=0, tiled=True)
    picked = returned.reshape(EXPERTS * CAP, D)[slot_index].reshape(-1, 2, D)
    layer_out = jnp.sum(shares[:, :, None] * picked.astype(jnp.float32), axis=1).astype(
        jnp.bfloat16
    )
    picked_grad = (
        returned_grad.reshape(EXPERTS * CAP, D)[slot_index].reshape(-1, 2, D).astype(jnp.float32)
    )
    grad_tokens = (picked_grad[:, 0] + picked_grad[:, 1]).astype(jnp.bfloat16)
    term_gate = jnp.einsum(
        "aserd,aserh->deh", received, gate_grad, preferred_element_type=jnp.float32
    )
    term_up = jnp.einsum("aserd,aserh->deh", received, up_grad, preferred_element_type=jnp.float32)
    term_down = jnp.einsum("aserh,aserd->hed", hidden, routed, preferred_element_type=jnp.float32)
    grad_gate, grad_up, grad_down = (
        lax.psum_scatter(
            term_gate.astype(jnp.bfloat16), "dp", scatter_dimension=0, tiled=True
        ).astype(jnp.float32),
        lax.psum_scatter(
            term_up.astype(jnp.bfloat16), "dp", scatter_dimension=0, tiled=True
        ).astype(jnp.float32),
        lax.psum_scatter(
            term_down.astype(jnp.bfloat16), "dp", scatter_dimension=0, tiled=True
        ).astype(jnp.float32),
    )
    grad_w_gate = grad_gate.transpose(1, 0, 2)
    grad_w_up = grad_up.transpose(1, 0, 2)
    grad_w_down = grad_down.transpose(1, 0, 2)
    return (layer_out, grad_tokens, grad_w_gate, grad_w_up, grad_w_down)


def solution(mesh):
    return jax.shard_map(
        per_device,
        mesh=mesh,
        in_specs=(
            P(("dp", "expert"), None),
            P(("dp", "expert"), None),
            P(("dp", "expert")),
            P(("dp", "expert"), None),
            P("expert", None, None),
            P("expert", None, None),
            P("expert", None, None),
        ),
        out_specs=(
            P(("dp", "expert"), None),
            P(("dp", "expert"), None),
            P("expert", "dp", None),
            P("expert", "dp", None),
            P("expert", "dp", None),
        ),
        check_vma=False,
    )
```

profile of v0, /device:TPU:1, one launch (start us, length us, event | category | flops | bytes accessed | tf_op | source)
XLA Modules:
  0.0 498.9 jit_solution(7771297061632297615)
XLA Ops:
  14.8 3.7 mul.78
  18.6 5.5 %scatter_custom_fusion.1 = bf16[1280,1024]{1,0:T(8,128)(2,1)} fusion(s32[512]{0:T(512)S(1)} %bitcast.190, bf16[]{:T(256)} %constant.9.clone.1, f32[512,1024]{1,0:T(8,128)} %mul.78, f32[512]{0:T(512)S(1)} %mul.75), kind=kCustom, calls=%fused_computation.60 | custom fusion | flops 1048576 | bytes 4720642 | tf_op jit(solution)/shard_map/scatter | solution.py:60
  24.1 7.4 %all-to-all-start.2 = ((bf16[16,1,2,40,1024]{4,3,2,1,0:T(8,128)(2,1)}), bf16[16,1,2,40,1024]{4,3,2,1,0:T(8,128)(2,1)}, u32[]{:S(2)}, u32[]{:S(2)}) async-start(bf16[16,1,2,40,1024]{4,3,2,1,0:T(8,128)(2,1)} %bitcast.189), calls=%async_computation.2 | async-start | bytes 5242880 | tf_op jit(solution)/shard_map/all_to_all | solution.py:71
  34.3 5.1 %scatter_custom_fusion = bf16[1280,1024]{1,0:T(8,128)(2,1)} fusion(s32[512]{0:T(512)S(1)} %bitcast.191, bf16[512,1024]{1,0:T(8,128)(2,1)} %reshape.169, bf16[]{:T(256)} %constant.9.clone.1), kind=kCustom, calls=%fused_computation.62 | custom fusion | bytes 2621952 | tf_op jit(solution)/shard_map/scatter | solution.py:59
  39.5 25.0 %all-to-all-done.2 = bf16[16,1,2,40,1024]{4,3,2,1,0:T(8,128)(2,1)} async-done(((bf16[16,1,2,40,1024]{4,3,2,1,0:T(8,128)(2,1)}), bf16[16,1,2,40,1024]{4,3,2,1,0:T(8,128)(2,1)}, u32[]{:S(2)}, u32[]{:S(2)}) %all-to-all-start.2) | async-done | bytes 2621472 | tf_op jit(solution)/shard_map/all_to_all | solution.py:71
  64.4 5.0 %all-to-all-start = ((bf16[16,1,2,40,1024]{4,3,2,1,0:T(8,128)(2,1)}), bf16[16,1,2,40,1024]{4,3,2,1,0:T(8,128)(2,1)}, u32[]{:S(2)}, u32[]{:S(2)}) async-start(bf16[16,1,2,40,1024]{4,3,2,1,0:T(8,128)(2,1)} %bitcast.188), calls=%async_computation | async-start | bytes 5242880 | tf_op jit(solution)/shard_map/all_to_all | solution.py:61
  69.7 5.4 %fusion.8 = f32[2,16,40,512]{3,2,1,0:T(8,128)} fusion(bf16[16,1,2,40,1024]{4,3,2,1,0:T(8,128)(2,1)} %all-to-all-done.2, bf16[2,512,1024]{2,1,0:T(8,128)(2,1)} %param.13), kind=kOutput, calls=%fused_computation.19 | convolution fusion | flops 1342177280 | bytes 7340032 | tf_op jit(solution)/shard_map/aserd,ehd->aserh/dot_general | solution.py:32
  75.1 27.3 %all-to-all-done = bf16[16,1,2,40,1024]{4,3,2,1,0:T(8,128)(2,1)} async-done(((bf16[16,1,2,40,1024]{4,3,2,1,0:T(8,128)(2,1)}), bf16[16,1,2,40,1024]{4,3,2,1,0:T(8,128)(2,1)}, u32[]{:S(2)}, u32[]{:S(2)}) %all-to-all-start) | async-done | bytes 2621472 | tf_op jit(solution)/shard_map/all_to_all | solution.py:61
  102.4 4.1 fusion.18
  106.5 5.5 %fusion.48 = (bf16[16,2,40,512]{3,2,0,1:T(8,128)(2,1)S(1)}, bf16[1,16,2,40,512]{4,3,1,2,0:T(8,128)(2,1)}, bf16[16,2,40,512]{3,2,0,1:T(8,128)(2,1)S(1)}) fusion(f32[2,16,40,512]{3,2,1,0:T(8,128)S(1)} %copy-done.6, f32[2,16,40,512]{3,2,1,0:T(8,128)S(1)} %fusion.18, bf16[2,1024,512]{2,1,0:T(8,128)(2,1)S(1)} %copy-done, ...), kind=kOutput, calls=%fused_computation.57 | convolution fusion | flops 1352007680 | bytes 13893632 | tf_op jit(solution)/shard_map/aserd,edh->aserh/dot_general | solution.py:19
  113.1 5.0 fusion.26
  118.1 6.3 %copy.48 = bf16[512,2,1024]{2,1,0:T(2,128)(2,1)} copy(bf16[512,2,1024]{0,2,1:T(8,128)(2,1)} %fusion.26) | data formatting | bytes 4194304 | tf_op jit(solution)/shard_map/convert_element_type | solution.py:97
  124.4 5.3 %fusion.29 = f32[2,16,40,1024]{3,2,1,0:T(8,128)} fusion(bf16[2,1024,512]{2,1,0:T(8,128)(2,1)S(1)} %copy-done, bf16[1,16,2,40,512]{4,3,1,2,0:T(8,128)(2,1)} %get-tuple-element.24), kind=kOutput, calls=%fused_computation.44 | convolution fusion | flops 1342177280 | bytes 8650752 | tf_op jit(solution)/shard_map/aserh,edh->aserd/dot_general | solution.py:39
  129.6 3.6 fusion.24
  133.2 4.1 copy.46
  140.9 4.0 copy.47
  146.5 4.0 fusion
  152.3 4.4 all-to-all-start.3
  156.7 3.7 convert_bitcast_fusion
  162.1 85.0 %all-to-all-done.3 = bf16[1,16,2,40,1024]{4,3,2,0,1:T(8,128)(2,1)S(1)} async-done(((bf16[1,16,2,40,1024]{4,3,2,0,1:T(8,128)(2,1)}), bf16[1,16,2,40,1024]{4,3,2,0,1:T(8,128)(2,1)S(1)}, u32[]{:S(2)}, u32[]{:S(2)}) %all-to-all-start.3) | async-done | bytes 2621472 | tf_op jit(solution)/shard_map/all_to_all | solution.py:75
  247.2 4.8 all-to-all-start.1
  259.0 84.3 %all-to-all-done.1 = bf16[1,16,2,40,1024]{4,3,2,0,1:T(8,128)(2,1)} async-done(((bf16[1,16,2,40,1024]{4,3,2,0,1:T(8,128)(2,1)}), bf16[1,16,2,40,1024]{4,3,2,0,1:T(8,128)(2,1)}, u32[]{:S(2)}, u32[]{:S(2)}) %all-to-all-start.1) | async-done | bytes 2621472 | tf_op jit(solution)/shard_map/all_to_all | solution.py:63
  343.4 4.8 gather_fusion
  356.7 130.9 %all-reduce.6.cloned.1.call-done = (bf16[1024,2,512]{2,1,0:T(2,128)(2,1)}, bf16[1024,2,512]{2,1,0:T(2,128)(2,1)}, bf16[512,2,1024]{2,1,0:T(2,128)(2,1)}) async-done(((bf16[1024,2,512]{2,1,0:T(2,128)(2,1)}, bf16[1024,2,512]{2,1,0:T(2,128)(2,1)}, bf16[512,2,1024]{2,1,0:T(2,128)(2,1)}), (bf16[1024,2,512]{2,1,0:T(2,128)(2,1)}, bf16[1024,2,512]{2,1,0:T(2,128)(2,1)}, ...) | async-done | bytes 6291472
  (54 shorter events, 39.1 us)
Async XLA Ops:
  7.2 99.3 %copy-start = (bf16[2,1024,512]{2,1,0:T(8,128)(2,1)S(1)}, bf16[2,1024,512]{2,1,0:T(8,128)(2,1)}, u32[]{:S(2)}) copy-start(bf16[2,1024,512]{2,1,0:T(8,128)(2,1)} %param.11) | copy-start | bytes 6291460
  24.1 40.3 %all-to-all-start.2 = ((bf16[16,1,2,40,1024]{4,3,2,1,0:T(8,128)(2,1)}), bf16[16,1,2,40,1024]{4,3,2,1,0:T(8,128)(2,1)}, u32[]{:S(2)}, u32[]{:S(2)}) async-start(bf16[16,1,2,40,1024]{4,3,2,1,0:T(8,128)(2,1)} %bitcast.189), calls=%async_computation.2 | async-start | bytes 5242880 | tf_op jit(solution)/shard_map/all_to_all | solution.py:71
  64.4 38.0 %all-to-all-start = ((bf16[16,1,2,40,1024]{4,3,2,1,0:T(8,128)(2,1)}), bf16[16,1,2,40,1024]{4,3,2,1,0:T(8,128)(2,1)}, u32[]{:S(2)}, u32[]{:S(2)}) async-start(bf16[16,1,2,40,1024]{4,3,2,1,0:T(8,128)(2,1)} %bitcast.188), calls=%async_computation | async-start | bytes 5242880 | tf_op jit(solution)/shard_map/all_to_all | solution.py:61
  69.5 418.2 %all-reduce.6.cloned.1.call-start = ((), (), s32[]{:S(2)}) async-start(), calls=%async_computation.4 | async-start | bytes 12582912
  102.4 4.1 copy-start.6
  112.0 1.1 copy-start.7
  124.4 5.3 %copy-start.4 = (bf16[1,16,2,40,512]{4,3,1,2,0:T(8,128)(2,1)S(1)}, bf16[1,16,2,40,512]{4,3,1,2,0:T(8,128)(2,1)}, u32[]{:S(2)}) copy-start(bf16[1,16,2,40,512]{4,3,1,2,0:T(8,128)(2,1)} %get-tuple-element.24) | copy-start | bytes 3932164
  144.9 1.6 copy-start.3
  152.3 94.9 %all-to-all-start.3 = ((bf16[1,16,2,40,1024]{4,3,2,0,1:T(8,128)(2,1)}), bf16[1,16,2,40,1024]{4,3,2,0,1:T(8,128)(2,1)S(1)}, u32[]{:S(2)}, u32[]{:S(2)}) async-start(bf16[1,16,2,40,1024]{4,3,2,0,1:T(8,128)(2,1)} %copy.43), calls=%async_computation.3 | async-start | bytes 5242880 | tf_op jit(solution)/shard_map/all_to_all | solution.py:75
  162.1 89.9 %copy-start.5 = (u32[256]{0:T(256)S(1)}, u32[256]{0:T(256)}, u32[]{:S(2)}) copy-start(u32[256]{0:T(256)} %constant.26) | copy-start | bytes 3076
  247.2 96.2 %all-to-all-start.1 = ((bf16[1,16,2,40,1024]{4,3,2,0,1:T(8,128)(2,1)}), bf16[1,16,2,40,1024]{4,3,2,0,1:T(8,128)(2,1)}, u32[]{:S(2)}, u32[]{:S(2)}) async-start(bf16[1,16,2,40,1024]{4,3,2,0,1:T(8,128)(2,1)} %copy.39), calls=%async_computation.1 | async-start | bytes 5242880 | tf_op jit(solution)/shard_map/all_to_all | solution.py:63
  350.5 2.7 copy-start.2
  352.1 140.0 %copy-start.1 = (bf16[2,1024,512]{2,1,0:T(8,128)(2,1)S(1)}, bf16[2,1024,512]{2,1,0:T(8,128)(2,1)}, u32[]{:S(2)}) copy-start(bf16[2,1024,512]{2,1,0:T(8,128)(2,1)} %param.11) | copy-start | bytes 6291460
Sparse Core Ops, SparseCore 0:
  145.1 342.5 all-reduce.5
where the time goes:
time: 504 us; the launch traced here: 499 us
  waiting for transfers between devices  353 us (70%)
  local copies, waits for them, and re-layouts  53.9 us (11%)
  matrix products  40.1 us (8%)
  starting transfers between devices  21.9 us (4%)
  between operations  15.5 us (3%)
  other arithmetic  15 us (3%)
    unnamed x2, waiting for transfers between devices  131 us
    all_to_all x1, waiting for transfers between devices, per_device(): lax.all_to_all(input_grad, 'expert', split_axis=1, concat_axis=0, tiled=T...  85 us
    all_to_all x1, waiting for transfers between devices, per_device(): lax.all_to_all(expert_out, 'expert', split_axis=1, concat_axis=0, tiled=T...  84.3 us
    all_to_all x1, waiting for transfers between devices, per_device(): lax.all_to_all(send_tokens, 'expert', split_axis=0, concat_axis=1, tiled=...  27.3 us
    all_to_all x1, waiting for transfers between devices, per_device(): lax.all_to_all(send_grads, 'expert', split_axis=0, concat_axis=1, tiled=T...  25 us
  transfers between devices with their start and end apart: 5, of which 5 were waited for; matrix products, arithmetic and copies ran while one was open for 9% of the time, Pallas kernels for 0%

commit v1 on v0

v1 whole, which is shorter than its diff:
```python
import jax
import jax.numpy as jnp
from jax import lax
from jax.experimental import pallas as pl
from jax.experimental.pallas import tpu as pltpu
from jax.sharding import PartitionSpec as P

D = 1024
HID = 512
TOK = 256
CAP = 40
GROUPS = 16
CHUNKS = 2
ROWS = GROUPS * CAP
RING = 8
HI = 2
GATE_ROWS = D // RING // HI
DOWN_ROWS = HID // RING // HI
SHARD_ROWS = GATE_ROWS + DOWN_ROWS
VMEM = pl.BlockSpec(memory_space=pltpu.VMEM)
SMEM = pl.BlockSpec(memory_space=pltpu.SMEM)
BF16 = jnp.bfloat16
F32 = jnp.float32


def mm(a, b, dims=((1,), (0,))):
    return lax.dot_general(a, b, (dims, ((), ())), preferred_element_type=F32)


def slot_rows(ids_ref, quant_ref, chunk):
    first, second = ids_ref[0:1, :], ids_ref[1:2, :]
    expert = lax.broadcasted_iota(jnp.int32, (GROUPS, TOK), 0) * CHUNKS + chunk
    is_first = expert == first
    chosen = is_first | (expert == second)
    before = lax.broadcasted_iota(jnp.int32, (TOK, TOK), 0) < lax.broadcasted_iota(
        jnp.int32, (TOK, TOK), 1
    )
    rank = mm(
        jnp.where(chosen, 1.0, 0.0).astype(BF16), jnp.where(before, 1.0, 0.0).astype(BF16)
    )
    place = jnp.where(chosen, rank.astype(jnp.int32), -1)
    share = quant_ref[...].astype(F32) / 256.0
    share = jnp.where(is_first, share, 1.0 - share)
    row = lax.broadcasted_iota(jnp.int32, (CAP, TOK), 0)
    hit = [row == place[g : g + 1, :] for g in range(GROUPS)]
    plain = jnp.concatenate([jnp.where(h, 1.0, 0.0) for h in hit], axis=0)
    weighted = jnp.concatenate(
        [jnp.where(h, share[g : g + 1, :], 0.0) for g, h in enumerate(hit)], axis=0
    )
    return plain.astype(BF16), weighted.astype(BF16)


def pack_kernel(ids_ref, quant_ref, tokens_ref, cot_ref, *send_refs):
    for chunk, send_ref in enumerate(send_refs):
        plain, weighted = slot_rows(ids_ref, quant_ref, chunk)
        send_ref[:, 0] = mm(plain, tokens_ref[...]).reshape(GROUPS, CAP, D).astype(BF16)
        send_ref[:, 1] = mm(weighted, cot_ref[...]).reshape(GROUPS, CAP, D).astype(BF16)


def pack(ids, quant, tokens, cotangent):
    shape = jax.ShapeDtypeStruct((GROUPS, 2, CAP, D), BF16)
    return pl.pallas_call(
        pack_kernel,
        out_shape=[shape] * CHUNKS,
        in_specs=[VMEM] * 4,
        out_specs=[VMEM] * CHUNKS,
        compiler_params=pltpu.CompilerParams(vmem_limit_bytes=40 << 20),
        cost_estimate=pl.CostEstimate(
            flops=4 * CHUNKS * ROWS * TOK * D, bytes_accessed=7 << 20, transcendentals=0
        ),
        name="pack",
    )(ids, quant, tokens, cotangent)


def expert_kernel(z_ref, recv_ref, gate_ref, up_ref, down_ref, ret_ref, *refs):
    part_refs, (grad_gu, grad_down) = refs[:RING], refs[RING:]
    rows = recv_ref[:, 0].astype(F32).reshape(ROWS, D).astype(BF16)
    routed = recv_ref[:, 1].astype(F32).reshape(ROWS, D).astype(BF16)
    w_gate, w_up, w_down = gate_ref[0], up_ref[0], down_ref[0]
    gate_value = mm(rows, w_gate)
    up_value = mm(rows, w_up)
    sig = jax.nn.sigmoid(gate_value)
    act = gate_value * sig
    hidden = (act * up_value).astype(BF16)
    hidden_grad = mm(routed, w_down, ((1,), (1,)))
    gate_grad = (hidden_grad * up_value * sig * (1.0 + gate_value * (1.0 - sig))).astype(BF16)
    up_grad = (hidden_grad * act).astype(BF16)
    both = jnp.concatenate([gate_grad, up_grad], axis=1)
    grad_gu[...] = mm(rows, both, ((0,), (0,)))
    grad_down[...] = mm(hidden, routed, ((0,), (0,)))
    z = z_ref[0]
    for j, part_ref in enumerate(part_refs):
        owner = lax.rem(z + j, RING)
        for h in range(HI):
            at = pl.multiple_of((owner * HI + h) * GATE_ROWS, GATE_ROWS)
            part_ref[h, :GATE_ROWS] = grad_gu[pl.ds(at, GATE_ROWS), :].astype(BF16)
            at = pl.multiple_of((owner * HI + h) * DOWN_ROWS, DOWN_ROWS)
            part_ref[h, GATE_ROWS:] = grad_down[pl.ds(at, DOWN_ROWS), :].astype(BF16)
    ret_ref[:, 0] = mm(hidden, w_down).reshape(GROUPS, CAP, D).astype(BF16)
    input_grad = mm(gate_grad, w_gate, ((1,), (1,))) + mm(up_grad, w_up, ((1,), (1,)))
    ret_ref[:, 1] = input_grad.reshape(GROUPS, CAP, D).astype(BF16)


def expert(z, recv, w_gate, w_up, w_down, chunk):
    part = jax.ShapeDtypeStruct((HI, SHARD_ROWS, D), BF16)

    def whole(*shape):
        return pl.BlockSpec(shape, lambda i: (0,) * len(shape))

    def one(*shape):
        return pl.BlockSpec((1,) + shape, lambda i: (chunk, 0, 0))

    out = pl.pallas_call(
        expert_kernel,
        grid=(1,),
        out_shape=[jax.ShapeDtypeStruct((GROUPS, 2, CAP, D), BF16)] + [part] * RING,
        in_specs=[
            SMEM,
            whole(GROUPS, 2, CAP, D),
            one(D, HID),
            one(D, HID),
            one(HID, D),
        ],
        out_specs=[whole(GROUPS, 2, CAP, D)] + [whole(HI, SHARD_ROWS, D)] * RING,
        scratch_shapes=[pltpu.VMEM((D, 2 * HID), F32), pltpu.VMEM((HID, D), F32)],
        compiler_params=pltpu.CompilerParams(vmem_limit_bytes=56 << 20),
        cost_estimate=pl.CostEstimate(
            flops=18 * ROWS * D * HID, bytes_accessed=12 << 20, transcendentals=ROWS * HID
        ),
        name=f"expert_{chunk}",
    )(z, recv, w_gate, w_up, w_down)
    return out[0], out[1:]


def unpack_kernel(ids_ref, quant_ref, *refs):
    ret_refs, (layer_ref, grad_ref) = refs[:CHUNKS], refs[CHUNKS:]
    layer, grad = 0.0, 0.0
    for chunk, ret_ref in enumerate(ret_refs):
        plain, weighted = slot_rows(ids_ref, quant_ref, chunk)
        outs = ret_ref[:, 0].astype(F32).reshape(ROWS, D).astype(BF16)
        layer += mm(weighted, outs, ((0,), (0,)))
        grads = ret_ref[:, 1].astype(F32).reshape(ROWS, D).astype(BF16)
        grad += mm(plain, grads, ((0,), (0,)))
    layer_ref[...] = layer.astype(BF16)
    grad_ref[...] = grad.astype(BF16)


def unpack(ids, quant, returned):
    shape = jax.ShapeDtypeStruct((TOK, D), BF16)
    return pl.pallas_call(
        unpack_kernel,
        out_shape=[shape] * 2,
        in_specs=[VMEM] * (2 + CHUNKS),
        out_specs=[VMEM] * 2,
        compiler_params=pltpu.CompilerParams(vmem_limit_bytes=40 << 20),
        cost_estimate=pl.CostEstimate(
            flops=4 * CHUNKS * ROWS * TOK * D, bytes_accessed=7 << 20, transcendentals=0
        ),
        name="unpack",
    )(ids, quant, *returned)


def chain(parts, hops, sign):
    step = [(i, (i // HI + sign) % RING * HI + i % HI) for i in range(RING * HI)]
    held = parts[sign * hops % RING]
    for j in range(hops - 1, -1, -1):
        held = lax.ppermute(held, "dp", step)
        if j:
            held = (held.astype(F32) + parts[sign * j % RING].astype(F32)).astype(BF16)
    return held


def reduce_shards(parts, up_hops):
    arrived_up = chain(parts, up_hops, 1)
    arrived_down = chain(parts, RING - 1 - up_hops, -1)
    total = parts[0].astype(F32) + arrived_up.astype(F32) + arrived_down.astype(F32)
    hi = lax.axis_index("dp") % HI
    mine = lax.dynamic_index_in_dim(total, hi, 0, keepdims=False)
    other = lax.dynamic_index_in_dim(total, 1 - hi, 0, keepdims=False).astype(BF16)
    got = lax.ppermute(other, "dp", [(i, i ^ 1) for i in range(RING * HI)])
    return mine + got.astype(F32)


def per_device(tokens, expert_ids, gate_quant, cotangent, w_gate, w_up, w_down):
    ids, quant = expert_ids.T, gate_quant[None, :]
    z = (lax.axis_index("dp") // HI).astype(jnp.int32).reshape(1)
    sends = pack(ids, quant, tokens, cotangent)
    returned, shards = [], []
    for chunk, send in enumerate(sends):
        recv = lax.all_to_all(send, "expert", 0, 0, tiled=True)
        ret, parts = expert(z, recv, w_gate, w_up, w_down, chunk)
        returned.append(lax.all_to_all(ret, "expert", 0, 0, tiled=True))
        shards.append(reduce_shards(parts, 3 + chunk))
    layer_out, grad_tokens = unpack(ids, quant, returned)
    shards = jnp.stack(shards)
    return (
        layer_out,
        grad_tokens,
        shards[:, :GATE_ROWS, :HID],
        shards[:, :GATE_ROWS, HID:],
        shards[:, GATE_ROWS:, :],
    )


def solution(mesh):
    return jax.shard_map(
        per_device,
        mesh=mesh,
        in_specs=(
            P(("dp", "expert"), None),
            P(("dp", "expert"), None),
            P(("dp", "expert")),
            P(("dp", "expert"), None),
            P("expert", None, None),
            P("expert", None, None),
            P("expert", None, None),
        ),
        out_specs=(
            P(("dp", "expert"), None),
            P(("dp", "expert"), None),
            P("expert", "dp", None),
            P("expert", "dp", None),
            P("expert", "dp", None),
        ),
        check_vma=False,
    )
```

time: 504 us -> 194 us (0.38)
  waiting for transfers between devices: 353 us -> 60.3 us
  local copies, waits for them, and re-layouts: 53.9 us -> 5.05 us
  matrix products: 40.1 us -> 0 us
  blocking collectives: 0 us -> 39.1 us
  Pallas kernels: 0 us -> 30.5 us
  starting transfers between devices: 21.9 us -> 42.5 us
  between operations: 15.5 us -> 0.87 us
    all_to_all x4 -> x3, waiting for transfers between devices: 222 us -> 21.5 us  [the longest x1 21.5 us: per_device(): recv = lax.all_to_all(send, 'expert', 0, 0, tiled=True)]
    unnamed x2 -> x0, waiting for transfers between devices: 131 us -> none
    dot_general x9 -> x0, matrix products: 40.1 us -> none  [the longest x1 5.5 us: expert_forward(): jnp.einsum('aserd,edh->aserh', received, w_gate, preferred_element_type=j...]
    all_to_all x0 -> x1, blocking collectives: none -> 39.1 us  [per_device(): recv = lax.all_to_all(send, 'expert', 0, 0, tiled=True)]
    ppermute x0 -> x16, waiting for transfers between devices: none -> 38.7 us  [the longest x14 27.7 us: chain(): held = lax.ppermute(held, 'dp', step)]
    pallas_call x0 -> x4, Pallas kernels: none -> 30.5 us  [the longest x2 22.6 us: expert(): pl.pallas_call(expert_kernel, grid=(1,), out_shape=[jax.ShapeDtypeStruct(...]
    ppermute x0 -> x16, starting transfers between devices: none -> 25.9 us  [the longest x14 20.9 us: chain(): held = lax.ppermute(held, 'dp', step)]
    convert_element_type x7 -> x2, local copies, waits for them, and re-layouts: 22.5 us -> 0.06 us  [reduce_shards(): lax.dynamic_index_in_dim(total, 1 - hi, 0, keepdims=False).astype(BF16)]
  transfers between devices with their start and end apart: 5 -> 19, of which waited for: 5 -> 10; matrix products, arithmetic and copies ran while one was open for 9% -> 8% of each run, Pallas kernels for 0% -> 12%
where the time goes in v1:
time: 194 us; the launch traced here: 193 us
  waiting for transfers between devices  60.3 us (31%)
  starting transfers between devices  42.5 us (22%)
  blocking collectives  39.1 us (20%)
  Pallas kernels  30.5 us (16%)
  other arithmetic  14.6 us (8%)
  local copies, waits for them, and re-layouts  5.05 us (3%)
    all_to_all x1, blocking collectives, per_device(): recv = lax.all_to_all(send, 'expert', 0, 0, tiled=True)  39.1 us
    ppermute x14, waiting for transfers between devices, chain(): held = lax.ppermute(held, 'dp', step)  27.7 us
    pallas_call x2, Pallas kernels, expert(): pl.pallas_call(expert_kernel, grid=(1,), out_shape=[jax.ShapeDtypeStruct(...  22.6 us
    all_to_all x1, waiting for transfers between devices, per_device(): recv = lax.all_to_all(send, 'expert', 0, 0, tiled=True)  21.5 us
    ppermute x14, starting transfers between devices, chain(): held = lax.ppermute(held, 'dp', step)  20.9 us
    all_to_all x2, starting transfers between devices, per_device(): returned.append(lax.all_to_all(ret, 'expert', 0, 0, tiled=True))  11.9 us
    ppermute x2, waiting for transfers between devices, reduce_shards(): got = lax.ppermute(other, 'dp', [(i, i ^ 1) for i in range(RING * HI)])  11 us
    convert_element_type x10, other arithmetic, chain(): held = (held.astype(F32) + parts[sign * j % RING].astype(F32)).astype(BF16)  10.3 us
  transfers between devices with their start and end apart: 19, of which 10 were waited for; matrix products, arithmetic and copies ran while one was open for 8% of the time, Pallas kernels for 12%

profile of v1, /device:TPU:1, one launch (start us, length us, event | category | flops | bytes accessed | tf_op | source)
XLA Modules:
  0.0 192.9 jit_solution(12563723492203676336)
XLA Ops:
  4.1 3.3 %pack.1 = (bf16[16,2,40,1024]{3,2,1,0:T(8,128)(2,1)S(1)}, bf16[16,2,40,1024]{3,2,1,0:T(8,128)(2,1)}) custom-call(s32[2,256]{1,0:T(2,128)S(1)} %bitcast.19, s32[1,256]{1,0:T(1,128)S(1)} %bitcast.21, bf16[256,1024]{1,0:T(8,128)(2,1)S(1)} %copy-done.4, bf16[256,1024]{1,0:T(8,128)(2,1)S(1)} %copy-done.5), custom_call_target="tpu_custom_call" | custom-call | flops 1342177280 | bytes 7340032 | tf_op jit(solution)/shard_map/pack/pallas_call | solution.py:62
  7.3 39.1 %all_to_all.20.recv_ref = bf16[16,2,40,1024]{3,2,1,0:T(8,128)(2,1)} all-to-all(bf16[16,2,40,1024]{3,2,1,0:T(8,128)(2,1)S(1)} %get-tuple-element.27), channel_id=1, replica_groups=mesh['dp'=16,'expert'=16] {'expert'}, dimensions={0} | all-to-all | bytes 5242880 | tf_op jit(solution)/shard_map/all_to_all | solution.py:190
  46.4 4.7 %all-to-all-start.2 = ((bf16[16,2,40,1024]{3,2,1,0:T(8,128)(2,1)}), bf16[16,2,40,1024]{3,2,1,0:T(8,128)(2,1)S(1)}, u32[]{:S(2)}, u32[]{:S(2)}) async-start(bf16[16,2,40,1024]{3,2,1,0:T(8,128)(2,1)} %get-tuple-element.29), calls=%async_computation.2 | async-start | bytes 5242880 | tf_op jit(solution)/shard_map/all_to_all | solution.py:190
  51.1 11.3 %expert_0.1 = (bf16[16,2,40,1024]{3,2,1,0:T(8,128)(2,1)}, bf16[2,96,1024]{2,1,0:T(8,128)(2,1)}, bf16[2,96,1024]{2,1,0:T(8,128)(2,1)}, bf16[2,96,1024]{2,1,0:T(8,...) custom-call(s32[1]{0:T(128)} %bitcast.2.z_ref, ...), custom_call_target="tpu_custom_call" | custom-call | flops 6039797760 | bytes 12582912 | tf_op jit(solution)/shard_map/expert_0/pallas_call | solution.py:113
  62.4 21.5 %all-to-all-done.2.recv_ref = bf16[16,2,40,1024]{3,2,1,0:T(8,128)(2,1)S(1)} async-done(((bf16[16,2,40,1024]{3,2,1,0:T(8,128)(2,1)}), bf16[16,2,40,1024]{3,2,1,0:T(8,128)(2,1)S(1)}, u32[]{:S(2)}, u32[]{:S(2)}) %all-to-all-start.2) | async-done | bytes 2621472 | tf_op jit(solution)/shard_map/all_to_all | solution.py:190
  85.4 4.4 %all-to-all-start.1 = ((bf16[16,2,40,1024]{3,2,1,0:T(8,128)(2,1)}), bf16[16,2,40,1024]{3,2,1,0:T(8,128)(2,1)S(1)}, u32[]{:S(2)}, u32[]{:S(2)}) async-start(bf16[16,2,40,1024]{3,2,1,0:T(8,128)(2,1)} %get-tuple-element.28), calls=%async_computation.1 | async-start | bytes 5242880 | tf_op jit(solution)/shard_map/all_to_all | solution.py:192
  89.8 11.3 %expert_1.1 = (bf16[16,2,40,1024]{3,2,1,0:T(8,128)(2,1)}, bf16[2,96,1024]{2,1,0:T(8,128)(2,1)}, bf16[2,96,1024]{2,1,0:T(8,128)(2,1)}, bf16[2,96,1024]{2,1,0:T(8,...) custom-call(s32[1]{0:T(128)} %bitcast.2.z_ref, ...), custom_call_target="tpu_custom_call" | custom-call | flops 6039797760 | bytes 12582912 | tf_op jit(solution)/shard_map/expert_1/pallas_call | solution.py:113
  102.9 4.0 %collective-permute-start.12 = (bf16[2,96,1024]{2,1,0:T(8,128)(2,1)}, bf16[2,96,1024]{2,1,0:T(8,128)(2,1)S(1)}, u32[]{:S(2)}, u32[]{:S(2)}) collective-permute-start(bf16[2,96,1024]{2,1,0:T(8,128)(2,1)} %get-tuple-element.46), channel_id=1, source_target_pairs={{0,224},{16,240},{32,0},{48,16},{64,32},{80,48},{96,64},{112,80},{... | collective-permute-start | bytes 1179656 | tf_op jit(solution)/shard_map/ppermute | solution.py:167
  106.9 2.7 %collective-permute-start.3 = (bf16[2,96,1024]{2,1,0:T(8,128)(2,1)S(1)}, bf16[2,96,1024]{2,1,0:T(8,128)(2,1)S(1)}, u32[]{:S(2)}, u32[]{:S(2)}) collective-permute-start(bf16[2,96,1024]{2,1,0:T(8,128)(2,1)S(1)} %copy-done.15), channel_id=1, source_target_pairs={{0,224},{16,240},{32,0},{48,16},{64,32},{80,48},{96,64},{112,80},{... | collective-permute-start | bytes 1179656 | tf_op jit(solution)/shard_map/ppermute | solution.py:167
  109.6 6.6 %collective-permute-done.8 = bf16[2,96,1024]{2,1,0:T(8,128)(2,1)S(1)} collective-permute-done((bf16[2,96,1024]{2,1,0:T(8,128)(2,1)}, bf16[2,96,1024]{2,1,0:T(8,128)(2,1)S(1)}, u32[]{:S(2)}, u32[]{:S(2)}) %collective-permute-start.8) | collective-permute-done | bytes 393248 | tf_op jit(solution)/shard_map/ppermute | solution.py:167
  118.6 2.7 %collective-permute-start.13 = (bf16[2,96,1024]{2,1,0:T(8,128)(2,1)S(1)}, bf16[2,96,1024]{2,1,0:T(8,128)(2,1)S(1)}, u32[]{:S(2)}, u32[]{:S(2)}) collective-permute-start(bf16[2,96,1024]{2,1,0:T(8,128)(2,1)S(1)} %add_convert_fusion.1), channel_id=1, source_target_pairs={{0,224},{16,240},{32,0},{48,16},{64,32},{80,48},{96,64},{112,80},{... | collective-permute-start | bytes 1179656 | tf_op jit(solution)/shard_map/ppermute | solution.py:167
  121.3 3.3 %collective-permute-done = bf16[2,96,1024]{2,1,0:T(8,128)(2,1)S(1)} collective-permute-done((bf16[2,96,1024]{2,1,0:T(8,128)(2,1)S(1)}, bf16[2,96,1024]{2,1,0:T(8,128)(2,1)S(1)}, u32[]{:S(2)}, u32[]{:S(2)}) %collective-permute-start) | collective-permute-done | bytes 393248 | tf_op jit(solution)/shard_map/ppermute | solution.py:167
  126.4 2.7 %collective-permute-start.4 = (bf16[2,96,1024]{2,1,0:T(8,128)(2,1)}, bf16[2,96,1024]{2,1,0:T(8,128)(2,1)}, u32[]{:S(2)}, u32[]{:S(2)}) collective-permute-start(bf16[2,96,1024]{2,1,0:T(8,128)(2,1)} %add_convert_fusion.7), channel_id=1, source_target_pairs={{0,224},{16,240},{32,0},{48,16},{64,32},{80,48},{96,64},{112,80},{... | collective-permute-start | bytes 1179656 | tf_op jit(solution)/shard_map/ppermute | solution.py:167
  129.1 4.0 %collective-permute-done.9 = bf16[2,96,1024]{2,1,0:T(8,128)(2,1)S(1)} collective-permute-done((bf16[2,96,1024]{2,1,0:T(8,128)(2,1)S(1)}, bf16[2,96,1024]{2,1,0:T(8,128)(2,1)S(1)}, u32[]{:S(2)}, u32[]{:S(2)}) %collective-permute-start.9) | collective-permute-done | bytes 393248 | tf_op jit(solution)/shard_map/ppermute | solution.py:167
  134.9 2.7 %collective-permute-start.14 = (bf16[2,96,1024]{2,1,0:T(8,128)(2,1)}, bf16[2,96,1024]{2,1,0:T(8,128)(2,1)}, u32[]{:S(2)}, u32[]{:S(2)}) collective-permute-start(bf16[2,96,1024]{2,1,0:T(8,128)(2,1)} %add_convert_fusion), channel_id=1, source_target_pairs={{0,224},{16,240},{32,0},{48,16},{64,32},{80,48},{96,64},{112,80},{... | collective-permute-start | bytes 1179656 | tf_op jit(solution)/shard_map/ppermute | solution.py:167
  137.5 7.5 %all-to-all-start.3 = ((bf16[16,2,40,1024]{3,2,1,0:T(8,128)(2,1)}), bf16[16,2,40,1024]{3,2,1,0:T(8,128)(2,1)}, u32[]{:S(2)}, u32[]{:S(2)}) async-start(bf16[16,2,40,1024]{3,2,1,0:T(8,128)(2,1)} %get-tuple-element.30), calls=%async_computation.3 | async-start | bytes 5242880 | tf_op jit(solution)/shard_map/all_to_all | solution.py:192
  146.9 3.1 %collective-permute-done.10 = bf16[2,96,1024]{2,1,0:T(8,128)(2,1)} collective-permute-done((bf16[2,96,1024]{2,1,0:T(8,128)(2,1)}, bf16[2,96,1024]{2,1,0:T(8,128)(2,1)}, u32[]{:S(2)}, u32[]{:S(2)}) %collective-permute-start.10) | collective-permute-done | bytes 393248 | tf_op jit(solution)/shard_map/ppermute | solution.py:167
  153.3 4.1 %collective-permute-done.5 = bf16[2,96,1024]{2,1,0:T(8,128)(2,1)S(1)} collective-permute-done((bf16[2,96,1024]{2,1,0:T(8,128)(2,1)S(1)}, bf16[2,96,1024]{2,1,0:T(8,128)(2,1)S(1)}, u32[]{:S(2)}, u32[]{:S(2)}) %collective-permute-start.5) | collective-permute-done | bytes 393248 | tf_op jit(solution)/shard_map/ppermute | solution.py:167
  157.5 3.6 %collective-permute-start.6 = (bf16[2,96,1024]{2,1,0:T(8,128)(2,1)S(1)}, bf16[2,96,1024]{2,1,0:T(8,128)(2,1)}, u32[]{:S(2)}, u32[]{:S(2)}) collective-permute-start(bf16[2,96,1024]{2,1,0:T(8,128)(2,1)S(1)} %add_convert_fusion.5), channel_id=1, source_target_pairs={{0,224},{16,240},{32,0},{48,16},{64,32},{80,48},{96,64},{112,80},{... | collective-permute-start | bytes 1179656 | tf_op jit(solution)/shard_map/ppermute | solution.py:167
  164.7 2.5 %collective-permute-start.15 = (bf16[96,1024]{1,0:T(8,128)(2,1)S(1)}, bf16[96,1024]{1,0:T(8,128)(2,1)S(1)}, u32[]{:S(2)}, u32[]{:S(2)}) collective-permute-start(bf16[96,1024]{1,0:T(8,128)(2,1)S(1)} %fusion.5), channel_id=1, source_target_pairs={{0,16},{16,0},{32,48},{48,32},{64,80},{80,64},{96,112},{112,96},{1... | collective-permute-start | bytes 589832 | tf_op jit(solution)/shard_map/ppermute | solution.py:180
  167.2 4.4 %collective-permute-done.2 = bf16[2,96,1024]{2,1,0:T(8,128)(2,1)} collective-permute-done((bf16[2,96,1024]{2,1,0:T(8,128)(2,1)S(1)}, bf16[2,96,1024]{2,1,0:T(8,128)(2,1)}, u32[]{:S(2)}, u32[]{:S(2)}) %collective-permute-start.2) | collective-permute-done | bytes 393248 | tf_op jit(solution)/shard_map/ppermute | solution.py:167
  175.6 6.9 %collective-permute-done.15 = bf16[96,1024]{1,0:T(8,128)(2,1)S(1)} collective-permute-done((bf16[96,1024]{1,0:T(8,128)(2,1)S(1)}, bf16[96,1024]{1,0:T(8,128)(2,1)S(1)}, u32[]{:S(2)}, u32[]{:S(2)}) %collective-permute-start.15) | collective-permute-done | bytes 196640 | tf_op jit(solution)/shard_map/ppermute | solution.py:180
  182.5 4.2 %collective-permute-done.7 = bf16[96,1024]{1,0:T(8,128)(2,1)S(1)} collective-permute-done((bf16[96,1024]{1,0:T(8,128)(2,1)S(1)}, bf16[96,1024]{1,0:T(8,128)(2,1)S(1)}, u32[]{:S(2)}, u32[]{:S(2)}) %collective-permute-start.7) | collective-permute-done | bytes 196640 | tf_op jit(solution)/shard_map/ppermute | solution.py:180
  188.3 4.6 %unpack.1 = (bf16[256,1024]{1,0:T(8,128)(2,1)}, bf16[256,1024]{1,0:T(8,128)(2,1)}) custom-call(s32[2,256]{1,0:T(2,128)S(1)} %bitcast.20, s32[1,256]{1,0:T(1,128)S(1)} %bitcast.22, bf16[16,2,40,1024]{3,2,1,0:T(8,128)(2,1)S(1)} %all-to-all-done.1.refs_0_, bf16[16,2,40,1024]{3,2,1,0:T(8,128)(2,1)} %all-to-all-done.3.refs_1_), custom_call_target="tpu_custom_call" | custom-call | flops 1342177280 | bytes 7340032 | tf_op jit(solution)/shard_map/unpack/pallas_call | solution.py:150
  (71 shorter events, 26.9 us)
Async XLA Ops:
  46.4 37.5 %all-to-all-start.2 = ((bf16[16,2,40,1024]{3,2,1,0:T(8,128)(2,1)}), bf16[16,2,40,1024]{3,2,1,0:T(8,128)(2,1)S(1)}, u32[]{:S(2)}, u32[]{:S(2)}) async-start(bf16[16,2,40,1024]{3,2,1,0:T(8,128)(2,1)} %get-tuple-element.29), calls=%async_computation.2 | async-start | bytes 5242880 | tf_op jit(solution)/shard_map/all_to_all | solution.py:190
  85.4 52.1 %all-to-all-start.1 = ((bf16[16,2,40,1024]{3,2,1,0:T(8,128)(2,1)}), bf16[16,2,40,1024]{3,2,1,0:T(8,128)(2,1)S(1)}, u32[]{:S(2)}, u32[]{:S(2)}) async-start(bf16[16,2,40,1024]{3,2,1,0:T(8,128)(2,1)} %get-tuple-element.28), calls=%async_computation.1 | async-start | bytes 5242880 | tf_op jit(solution)/shard_map/all_to_all | solution.py:192
  89.8 17.1 %copy-start.16 = (bf16[2,96,1024]{2,1,0:T(8,128)(2,1)S(1)}, bf16[2,96,1024]{2,1,0:T(8,128)(2,1)}, u32[]{:S(2)}) copy-start(bf16[2,96,1024]{2,1,0:T(8,128)(2,1)} %get-tuple-element.34) | copy-start | bytes 1179652
  89.8 17.1 %copy-start.15 = (bf16[2,96,1024]{2,1,0:T(8,128)(2,1)S(1)}, bf16[2,96,1024]{2,1,0:T(8,128)(2,1)}, u32[]{:S(2)}) copy-start(bf16[2,96,1024]{2,1,0:T(8,128)(2,1)} %get-tuple-element.37) | copy-start | bytes 1179652
  101.1 23.5 %copy-start.12 = (bf16[2,96,1024]{2,1,0:T(8,128)(2,1)S(1)}, bf16[2,96,1024]{2,1,0:T(8,128)(2,1)}, u32[]{:S(2)}) copy-start(bf16[2,96,1024]{2,1,0:T(8,128)(2,1)} %get-tuple-element.35) | copy-start | bytes 1179652
  101.2 24.4 %copy-start.10 = (bf16[2,96,1024]{2,1,0:T(8,128)(2,1)S(1)}, bf16[2,96,1024]{2,1,0:T(8,128)(2,1)}, u32[]{:S(2)}) copy-start(bf16[2,96,1024]{2,1,0:T(8,128)(2,1)} %get-tuple-element.38) | copy-start | bytes 1179652
  101.2 31.9 %copy-start.13 = (bf16[2,96,1024]{2,1,0:T(8,128)(2,1)S(1)}, bf16[2,96,1024]{2,1,0:T(8,128)(2,1)}, u32[]{:S(2)}) copy-start(bf16[2,96,1024]{2,1,0:T(8,128)(2,1)} %get-tuple-element.44) | copy-start | bytes 1179652
  101.2 15.0 %collective-permute-start.8 = (bf16[2,96,1024]{2,1,0:T(8,128)(2,1)}, bf16[2,96,1024]{2,1,0:T(8,128)(2,1)S(1)}, u32[]{:S(2)}, u32[]{:S(2)}) collective-permute-start(bf16[2,96,1024]{2,1,0:T(8,128)(2,1)} %get-tuple-element.42), channel_id=1, source_target_pairs={{0,32},{16,48},{32,64},{48,80},{64,96},{80,112},{96,128},{112,144}... | collective-permute-start | bytes 1179656 | tf_op jit(solution)/shard_map/ppermute | solution.py:167
  102.9 14.5 %collective-permute-start.12 = (bf16[2,96,1024]{2,1,0:T(8,128)(2,1)}, bf16[2,96,1024]{2,1,0:T(8,128)(2,1)S(1)}, u32[]{:S(2)}, u32[]{:S(2)}) collective-permute-start(bf16[2,96,1024]{2,1,0:T(8,128)(2,1)} %get-tuple-element.46), channel_id=1, source_target_pairs={{0,224},{16,240},{32,0},{48,16},{64,32},{80,48},{96,64},{112,80},{... | collective-permute-start | bytes 1179656 | tf_op jit(solution)/shard_map/ppermute | solution.py:167
  106.9 17.7 %collective-permute-start = (bf16[2,96,1024]{2,1,0:T(8,128)(2,1)S(1)}, bf16[2,96,1024]{2,1,0:T(8,128)(2,1)S(1)}, u32[]{:S(2)}, u32[]{:S(2)}) collective-permute-start(bf16[2,96,1024]{2,1,0:T(8,128)(2,1)S(1)} %copy-done.16), channel_id=1, source_target_pairs={{0,32},{16,48},{32,64},{48,80},{64,96},{80,112},{96,128},{112,144}... | collective-permute-start | bytes 1179656 | tf_op jit(solution)/shard_map/ppermute | solution.py:167
  106.9 18.6 %collective-permute-start.3 = (bf16[2,96,1024]{2,1,0:T(8,128)(2,1)S(1)}, bf16[2,96,1024]{2,1,0:T(8,128)(2,1)S(1)}, u32[]{:S(2)}, u32[]{:S(2)}) collective-permute-start(bf16[2,96,1024]{2,1,0:T(8,128)(2,1)S(1)} %copy-done.15), channel_id=1, source_target_pairs={{0,224},{16,240},{32,0},{48,16},{64,32},{80,48},{96,64},{112,80},{... | collective-permute-start | bytes 1179656 | tf_op jit(solution)/shard_map/ppermute | solution.py:167
  117.3 15.7 %collective-permute-start.9 = (bf16[2,96,1024]{2,1,0:T(8,128)(2,1)S(1)}, bf16[2,96,1024]{2,1,0:T(8,128)(2,1)S(1)}, u32[]{:S(2)}, u32[]{:S(2)}) collective-permute-start(bf16[2,96,1024]{2,1,0:T(8,128)(2,1)S(1)} %add_convert_fusion.4), channel_id=1, source_target_pairs={{0,32},{16,48},{32,64},{48,80},{64,96},{80,112},{96,128},{112,144}... | collective-permute-start | bytes 1179656 | tf_op jit(solution)/shard_map/ppermute | solution.py:167
  118.6 15.3 %collective-permute-start.13 = (bf16[2,96,1024]{2,1,0:T(8,128)(2,1)S(1)}, bf16[2,96,1024]{2,1,0:T(8,128)(2,1)S(1)}, u32[]{:S(2)}, u32[]{:S(2)}) collective-permute-start(bf16[2,96,1024]{2,1,0:T(8,128)(2,1)S(1)} %add_convert_fusion.1), channel_id=1, source_target_pairs={{0,224},{16,240},{32,0},{48,16},{64,32},{80,48},{96,64},{112,80},{... | collective-permute-start | bytes 1179656 | tf_op jit(solution)/shard_map/ppermute | solution.py:167
  125.5 26.5 %collective-permute-start.1 = (bf16[2,96,1024]{2,1,0:T(8,128)(2,1)}, bf16[2,96,1024]{2,1,0:T(8,128)(2,1)}, u32[]{:S(2)}, u32[]{:S(2)}) collective-permute-start(bf16[2,96,1024]{2,1,0:T(8,128)(2,1)} %add_convert_fusion.9), channel_id=1, source_target_pairs={{0,32},{16,48},{32,64},{48,80},{64,96},{80,112},{96,128},{112,144}... | collective-permute-start | bytes 1179656 | tf_op jit(solution)/shard_map/ppermute | solution.py:167
  126.4 18.6 %collective-permute-start.4 = (bf16[2,96,1024]{2,1,0:T(8,128)(2,1)}, bf16[2,96,1024]{2,1,0:T(8,128)(2,1)}, u32[]{:S(2)}, u32[]{:S(2)}) collective-permute-start(bf16[2,96,1024]{2,1,0:T(8,128)(2,1)} %add_convert_fusion.7), channel_id=1, source_target_pairs={{0,224},{16,240},{32,0},{48,16},{64,32},{80,48},{96,64},{112,80},{... | collective-permute-start | bytes 1179656 | tf_op jit(solution)/shard_map/ppermute | solution.py:167
  134.0 16.1 %collective-permute-start.10 = (bf16[2,96,1024]{2,1,0:T(8,128)(2,1)}, bf16[2,96,1024]{2,1,0:T(8,128)(2,1)}, u32[]{:S(2)}, u32[]{:S(2)}) collective-permute-start(bf16[2,96,1024]{2,1,0:T(8,128)(2,1)} %add_convert_fusion.3), channel_id=1, source_target_pairs={{0,32},{16,48},{32,64},{48,80},{64,96},{80,112},{96,128},{112,144}... | collective-permute-start | bytes 1179656 | tf_op jit(solution)/shard_map/ppermute | solution.py:167
  134.9 26.2 %collective-permute-start.14 = (bf16[2,96,1024]{2,1,0:T(8,128)(2,1)}, bf16[2,96,1024]{2,1,0:T(8,128)(2,1)}, u32[]{:S(2)}, u32[]{:S(2)}) collective-permute-start(bf16[2,96,1024]{2,1,0:T(8,128)(2,1)} %add_convert_fusion), channel_id=1, source_target_pairs={{0,224},{16,240},{32,0},{48,16},{64,32},{80,48},{96,64},{112,80},{... | collective-permute-start | bytes 1179656 | tf_op jit(solution)/shard_map/ppermute | solution.py:167
  137.5 50.7 %all-to-all-start.3 = ((bf16[16,2,40,1024]{3,2,1,0:T(8,128)(2,1)}), bf16[16,2,40,1024]{3,2,1,0:T(8,128)(2,1)}, u32[]{:S(2)}, u32[]{:S(2)}) async-start(bf16[16,2,40,1024]{3,2,1,0:T(8,128)(2,1)} %get-tuple-element.30), calls=%async_computation.3 | async-start | bytes 5242880 | tf_op jit(solution)/shard_map/all_to_all | solution.py:192
  146.2 11.1 %collective-permute-start.5 = (bf16[2,96,1024]{2,1,0:T(8,128)(2,1)S(1)}, bf16[2,96,1024]{2,1,0:T(8,128)(2,1)S(1)}, u32[]{:S(2)}, u32[]{:S(2)}) collective-permute-start(bf16[2,96,1024]{2,1,0:T(8,128)(2,1)S(1)} %add_convert_fusion.6), channel_id=1, source_target_pairs={{0,224},{16,240},{32,0},{48,16},{64,32},{80,48},{96,64},{112,80},{... | collective-permute-start | bytes 1179656 | tf_op jit(solution)/shard_map/ppermute | solution.py:167
  152.0 11.2 %collective-permute-start.11 = (bf16[2,96,1024]{2,1,0:T(8,128)(2,1)}, bf16[2,96,1024]{2,1,0:T(8,128)(2,1)}, u32[]{:S(2)}, u32[]{:S(2)}) collective-permute-start(bf16[2,96,1024]{2,1,0:T(8,128)(2,1)} %add_convert_fusion.2), channel_id=1, source_target_pairs={{0,32},{16,48},{32,64},{48,80},{64,96},{80,112},{96,128},{112,144}... | collective-permute-start | bytes 1179656 | tf_op jit(solution)/shard_map/ppermute | solution.py:167
  153.2 18.5 %collective-permute-start.2 = (bf16[2,96,1024]{2,1,0:T(8,128)(2,1)S(1)}, bf16[2,96,1024]{2,1,0:T(8,128)(2,1)}, u32[]{:S(2)}, u32[]{:S(2)}) collective-permute-start(bf16[2,96,1024]{2,1,0:T(8,128)(2,1)S(1)} %add_convert_fusion.8), channel_id=1, source_target_pairs={{0,32},{16,48},{32,64},{48,80},{64,96},{80,112},{96,128},{112,144}... | collective-permute-start | bytes 1179656 | tf_op jit(solution)/shard_map/ppermute | solution.py:167
  157.5 14.2 %collective-permute-start.6 = (bf16[2,96,1024]{2,1,0:T(8,128)(2,1)S(1)}, bf16[2,96,1024]{2,1,0:T(8,128)(2,1)}, u32[]{:S(2)}, u32[]{:S(2)}) collective-permute-start(bf16[2,96,1024]{2,1,0:T(8,128)(2,1)S(1)} %add_convert_fusion.5), channel_id=1, source_target_pairs={{0,224},{16,240},{32,0},{48,16},{64,32},{80,48},{96,64},{112,80},{... | collective-permute-start | bytes 1179656 | tf_op jit(solution)/shard_map/ppermute | solution.py:167
  164.7 17.7 %collective-permute-start.15 = (bf16[96,1024]{1,0:T(8,128)(2,1)S(1)}, bf16[96,1024]{1,0:T(8,128)(2,1)S(1)}, u32[]{:S(2)}, u32[]{:S(2)}) collective-permute-start(bf16[96,1024]{1,0:T(8,128)(2,1)S(1)} %fusion.5), channel_id=1, source_target_pairs={{0,16},{16,0},{32,48},{48,32},{64,80},{80,64},{96,112},{112,96},{1... | collective-permute-start | bytes 589832 | tf_op jit(solution)/shard_map/ppermute | solution.py:180
  173.0 13.6 %collective-permute-start.7 = (bf16[96,1024]{1,0:T(8,128)(2,1)S(1)}, bf16[96,1024]{1,0:T(8,128)(2,1)S(1)}, u32[]{:S(2)}, u32[]{:S(2)}) collective-permute-start(bf16[96,1024]{1,0:T(8,128)(2,1)S(1)} %fusion.4), channel_id=1, source_target_pairs={{0,16},{16,0},{32,48},{48,32},{64,80},{80,64},{96,112},{112,96},{1... | collective-permute-start | bytes 589832 | tf_op jit(solution)/shard_map/ppermute | solution.py:180
  (12 other events, 97.1 us)

commit v2 on v1

v2 whole, which is shorter than its diff:
```python
import functools

import jax
import jax.numpy as jnp
from jax import lax
from jax.experimental import pallas as pl
from jax.experimental.pallas import tpu as pltpu
from jax.sharding import PartitionSpec as P

D = 1024
HID = 512
TOK = 256
CAP = 40
GROUPS = 16
CHUNKS = 2
ROWS = GROUPS * CAP
RING = 8
HI = 2
GATE_ROWS = D // RING // HI
DOWN_ROWS = HID // RING // HI
SHARD_ROWS = GATE_ROWS + DOWN_ROWS
VMEM = pl.BlockSpec(memory_space=pltpu.VMEM)
ANY = pl.BlockSpec(memory_space=pl.ANY)
SMEM = pl.BlockSpec(memory_space=pltpu.SMEM)
BF16 = jnp.bfloat16
F32 = jnp.float32


def mm(a, b, dims=((1,), (0,))):
    return lax.dot_general(a, b, (dims, ((), ())), preferred_element_type=F32)


def whole(*shape):
    return pl.BlockSpec(shape, lambda i: (0,) * len(shape))


def one(chunk, *shape):
    return pl.BlockSpec((1,) + shape, lambda i: (chunk, 0, 0))


def slot_rows(ids_ref, quant_ref, chunk):
    first, second = ids_ref[0:1, :], ids_ref[1:2, :]
    expert = lax.broadcasted_iota(jnp.int32, (GROUPS, TOK), 0) * CHUNKS + chunk
    is_first = expert == first
    chosen = is_first | (expert == second)
    before = lax.broadcasted_iota(jnp.int32, (TOK, TOK), 0) < lax.broadcasted_iota(
        jnp.int32, (TOK, TOK), 1
    )
    rank = mm(
        jnp.where(chosen, 1.0, 0.0).astype(BF16), jnp.where(before, 1.0, 0.0).astype(BF16)
    )
    place = jnp.where(chosen, rank.astype(jnp.int32), -1)
    share = quant_ref[...].astype(F32) / 256.0
    share = jnp.where(is_first, share, 1.0 - share)
    row = lax.broadcasted_iota(jnp.int32, (CAP, TOK), 0)
    hit = [row == place[g : g + 1, :] for g in range(GROUPS)]
    plain = jnp.concatenate([jnp.where(h, 1.0, 0.0) for h in hit], axis=0)
    weighted = jnp.concatenate(
        [jnp.where(h, share[g : g + 1, :], 0.0) for g, h in enumerate(hit)], axis=0
    )
    return plain.astype(BF16), weighted.astype(BF16)


def pack_kernel(chunk, ids_ref, quant_ref, tokens_ref, cot_ref, *refs):
    send_ref, plain_ref, weighted_ref = refs[-3:]

    @pl.when(pl.program_id(0) == 0)
    def _():
        plain_ref[...], weighted_ref[...] = slot_rows(ids_ref, quant_ref, chunk)

    width = tokens_ref.shape[1]
    rows = mm(plain_ref[...], tokens_ref[...])
    send_ref[:, 0] = rows.reshape(GROUPS, CAP, width).astype(BF16)
    rows = mm(weighted_ref[...], cot_ref[...])
    send_ref[:, 1] = rows.reshape(GROUPS, CAP, width).astype(BF16)


def pack(ids, quant, tokens, cotangent, chunk, after):
    steps = 4
    columns = pl.BlockSpec((TOK, D // steps), lambda i: (0, i))
    return pl.pallas_call(
        functools.partial(pack_kernel, chunk),
        grid=(steps,),
        out_shape=pltpu.HBM((GROUPS, 2, CAP, D), BF16),
        in_specs=[whole(2, TOK), whole(1, TOK), columns, columns] + [ANY] * len(after),
        out_specs=pl.BlockSpec((GROUPS, 2, CAP, D // steps), lambda i: (0, 0, 0, i)),
        scratch_shapes=[pltpu.VMEM((ROWS, TOK), BF16)] * 2,
        compiler_params=pltpu.CompilerParams(vmem_limit_bytes=(60 if chunk == 0 else 24) << 20),
        cost_estimate=pl.CostEstimate(
            flops=4 * ROWS * TOK * D, bytes_accessed=4 << 20, transcendentals=0
        ),
        name=f"pack_{chunk}",
    )(ids, quant, tokens, cotangent, *after)


def pick_kernel(ids_ref, quant_ref, *pick_refs):
    for chunk, pick_ref in enumerate(pick_refs):
        for kind, rows in enumerate(slot_rows(ids_ref, quant_ref, chunk)):
            pick_ref[kind] = rows.astype(F32).T.astype(BF16)


def picks(ids, quant):
    return pl.pallas_call(
        pick_kernel,
        grid=(1,),
        out_shape=[pltpu.HBM((2, TOK, ROWS), BF16)] * CHUNKS,
        in_specs=[whole(2, TOK), whole(1, TOK)],
        out_specs=[whole(2, TOK, ROWS)] * CHUNKS,
        compiler_params=pltpu.CompilerParams(vmem_limit_bytes=20 << 20),
        cost_estimate=pl.CostEstimate(
            flops=4 * TOK * TOK * GROUPS, bytes_accessed=2 << 20, transcendentals=0
        ),
        name="picks",
    )(ids, quant)


def expert_kernel(chunk, waits, z_ref, recv_ref, gate_ref, up_ref, down_ref, *refs):
    hidden_ref, grads_ref, *refs = refs[waits:]
    part_refs, (grad_gu, grad_down, *held, sems) = refs[:RING], refs[RING:]
    recv, w_gate, w_up, w_down = held
    sources = (recv_ref, gate_ref.at[chunk], up_ref.at[chunk], down_ref.at[chunk])
    loads = [
        pltpu.make_async_copy(source, to, sems.at[i])
        for i, (source, to) in enumerate(zip(sources, held))
    ]
    for load in loads:
        load.start()
    loads[0].wait()
    rows = recv[:, 0].astype(F32).reshape(ROWS, D).astype(BF16)
    routed = recv[:, 1].astype(F32).reshape(ROWS, D).astype(BF16)
    loads[1].wait()
    gate_value = mm(rows, w_gate[...])
    loads[2].wait()
    up_value = mm(rows, w_up[...])
    sig = jax.nn.sigmoid(gate_value)
    act = gate_value * sig
    hidden = (act * up_value).astype(BF16)
    loads[3].wait()
    hidden_grad = mm(routed, w_down[...], ((1,), (1,)))
    gate_grad = (hidden_grad * up_value * sig * (1.0 + gate_value * (1.0 - sig))).astype(BF16)
    up_grad = (hidden_grad * act).astype(BF16)
    both = jnp.concatenate([gate_grad, up_grad], axis=1)
    hidden_ref[...] = hidden
    grads_ref[...] = both
    grad_gu[...] = mm(rows, both, ((0,), (0,)))
    grad_down[...] = mm(hidden, routed, ((0,), (0,)))
    z = z_ref[0]
    for j, part_ref in enumerate(part_refs):
        owner = lax.rem(z + j, RING)
        for h in range(HI):
            at = pl.multiple_of((owner * HI + h) * GATE_ROWS, GATE_ROWS)
            part_ref[h, :GATE_ROWS] = grad_gu[pl.ds(at, GATE_ROWS), :].astype(BF16)
            at = pl.multiple_of((owner * HI + h) * DOWN_ROWS, DOWN_ROWS)
            part_ref[h, GATE_ROWS:] = grad_down[pl.ds(at, DOWN_ROWS), :].astype(BF16)


def held_in(space, *arrays):
    return [pltpu.with_memory_space_constraint(a, space) for a in arrays]


def expert(z, recv, w_gate, w_up, w_down, chunk, after):
    part = pltpu.VMEM((HI, SHARD_ROWS, D), BF16)
    weight = 3 if chunk else 1
    hidden, grads, *parts = pl.pallas_call(
        functools.partial(expert_kernel, chunk, len(after)),
        out_shape=[pltpu.VMEM((ROWS, HID), BF16), pltpu.VMEM((ROWS, 2 * HID), BF16)]
        + [part] * RING,
        in_specs=[SMEM] + [ANY] * (4 + len(after)),
        out_specs=[VMEM] * (2 + RING),
        scratch_shapes=[pltpu.VMEM((D, 2 * HID), F32), pltpu.VMEM((HID, D), F32)]
        + [pltpu.VMEM((GROUPS, 2, CAP, D), BF16)]
        + [pltpu.VMEM((D, HID), BF16)] * 2
        + [pltpu.VMEM((HID, D), BF16), pltpu.SemaphoreType.DMA((4,))],
        compiler_params=pltpu.CompilerParams(vmem_limit_bytes=27 << 20),
        cost_estimate=pl.CostEstimate(
            flops=weight * 12 * ROWS * D * HID,
            bytes_accessed=weight * 10 << 20,
            transcendentals=ROWS * HID,
        ),
        name=f"expert_{chunk}",
    )(z, *held_in(pltpu.HBM, recv, w_gate, w_up, w_down), *after)
    return hidden, grads, parts


def answer_kernel(hidden_ref, grads_ref, gate_ref, up_ref, down_ref, *refs):
    ret_ref = refs[-1]
    groups = ret_ref.shape[0]
    out = mm(hidden_ref[...], down_ref[0])
    ret_ref[:, 0] = out.reshape(groups, CAP, D).astype(BF16)
    input_grad = mm(grads_ref[:, :HID], gate_ref[0], ((1,), (1,)))
    input_grad += mm(grads_ref[:, HID:], up_ref[0], ((1,), (1,)))
    ret_ref[:, 1] = input_grad.reshape(groups, CAP, D).astype(BF16)


def answer(hidden, grads, w_gate, w_up, w_down, chunk, after):
    steps = 2
    return pl.pallas_call(
        answer_kernel,
        grid=(steps,),
        out_shape=pltpu.HBM((GROUPS, 2, CAP, D), BF16),
        in_specs=[
            pl.BlockSpec((ROWS // steps, HID), lambda i: (i, 0)),
            pl.BlockSpec((ROWS // steps, 2 * HID), lambda i: (i, 0)),
        ]
        + [one(chunk, D, HID), one(chunk, D, HID), one(chunk, HID, D)]
        + [ANY] * len(after),
        out_specs=pl.BlockSpec((GROUPS // steps, 2, CAP, D), lambda i: (i, 0, 0, 0)),
        compiler_params=pltpu.CompilerParams(vmem_limit_bytes=24 << 20),
        cost_estimate=pl.CostEstimate(
            flops=6 * ROWS * D * HID, bytes_accessed=8 << 20, transcendentals=0
        ),
        name=f"answer_{chunk}",
    )(hidden, grads, *held_in(pltpu.HBM, w_gate, w_up, w_down), *after)


def unpack_kernel(pick_ref, ret_ref, *refs):
    *earlier, layer_ref, grad_ref = refs
    width = layer_ref.shape[1]
    for kind, out_ref in ((0, layer_ref), (1, grad_ref)):
        rows = ret_ref[:, kind].astype(F32).reshape(ROWS, width).astype(BF16)
        total = mm(pick_ref[1 - kind], rows)
        if earlier:
            total += earlier[kind][...]
        out_ref[...] = total.astype(out_ref.dtype)


def unpack(pick, returned, chunk, earlier):
    steps = 2
    columns = pl.BlockSpec((TOK, D // steps), lambda i: (0, i))
    last = chunk == CHUNKS - 1
    return pl.pallas_call(
        unpack_kernel,
        grid=(steps,),
        out_shape=[jax.ShapeDtypeStruct((TOK, D), BF16 if last else F32)] * 2,
        in_specs=[
            whole(2, TOK, ROWS),
            pl.BlockSpec((GROUPS, 2, CAP, D // steps), lambda i: (0, 0, 0, i)),
        ]
        + [columns] * len(earlier),
        out_specs=[columns] * 2,
        compiler_params=pltpu.CompilerParams(vmem_limit_bytes=20 << 20),
        cost_estimate=pl.CostEstimate(
            flops=4 * ROWS * TOK * D, bytes_accessed=4 << 20, transcendentals=0
        ),
        name=f"unpack_{chunk}",
    )(*held_in(pltpu.HBM, pick, returned), *earlier)


def nothing(*refs):
    pass


def gate(array, *after):
    return pl.pallas_call(
        nothing,
        out_shape=pltpu.HBM(array.shape, array.dtype),
        in_specs=[ANY] * (1 + len(after)),
        out_specs=pl.BlockSpec(memory_space=pltpu.HBM),
        input_output_aliases={0: 0},
        cost_estimate=pl.CostEstimate(flops=0, bytes_accessed=0, transcendentals=0),
        name="gate",
    )(*held_in(pltpu.HBM, array), *after)


def ring_step(held, sign, across=0):
    step = [
        (i, (i // HI + sign) % RING * HI + (i + across) % HI) for i in range(RING * HI)
    ]
    return lax.ppermute(held, "dp", step)


def add_part(held, part):
    return (held.astype(F32) + part.astype(F32)).astype(BF16)


class Ring:
    def __init__(self, parts, up_hops):
        self.parts = parts
        self.hops = {1: up_hops, -1: RING - 1 - up_hops}
        self.held = {s: parts[s * n % RING] for s, n in self.hops.items()}

    def step(self, up=(), down=()):
        for sign, left in self.hops.items():
            if left:
                self.hops[sign] = left - 1
                held = ring_step(self.held[sign], sign)
                if left > 1:
                    part, *_ = lax.optimization_barrier(
                        (self.parts[sign * (left - 1) % RING], *(up if sign > 0 else down))
                    )
                    held = add_part(held, part)
                self.held[sign] = held

    def now(self):
        return self.held[1], self.held[-1]

    def before(self, *others):
        up, down, *others = lax.optimization_barrier((self.held[1], self.held[-1], *others))
        self.held = {1: up, -1: down}
        return others

    def finish(self):
        total = (
            self.parts[0].astype(F32) + self.held[1].astype(F32) + self.held[-1].astype(F32)
        )
        mine, other = halves(total)
        return mine + ring_step(other.astype(BF16), 0, 1).astype(F32)

    def finish_direct(self, sign):
        total = self.parts[0].astype(F32) + self.held[-sign].astype(F32)
        mine, other = halves(total)
        same, cross = halves(self.held[sign])
        arrived = [
            ring_step(same, sign),
            ring_step(cross, sign, 1),
            ring_step(other.astype(BF16), 0, 1),
        ]
        return mine + sum(a.astype(F32) for a in arrived)


def halves(pair):
    hi = lax.axis_index("dp") % HI
    return [lax.dynamic_index_in_dim(pair, h, 0, keepdims=False) for h in (hi, 1 - hi)]


def exchange(rows):
    return lax.all_to_all(rows, "expert", 0, 0, tiled=True)


def per_device(tokens, expert_ids, gate_quant, cotangent, w_gate, w_up, w_down):
    ids, quant = expert_ids.T, gate_quant[None, :]
    weights = (w_gate, w_up, w_down)
    z = (lax.axis_index("dp") // HI).astype(jnp.int32).reshape(1)
    pick = picks(ids, quant)
    recv_0 = exchange(pack(ids, quant, tokens, cotangent, 0, ()))
    recv_1 = exchange(pack(ids, quant, tokens, cotangent, 1, pick))
    hidden_0, grads_0, parts_0 = expert(z, recv_0, *weights, 0, ())
    ring_0 = Ring(parts_0, 3)
    ret_0 = answer(hidden_0, grads_0, *weights, 0, ())
    ring_0.step()
    back_0 = exchange(gate(ret_0, *ring_0.now()))
    ring_0.step()
    hidden_1, grads_1, parts_1 = expert(z, recv_1, *weights, 1, ring_0.now())
    ring_1 = Ring(parts_1, 4)
    ring_1.step()
    ret_1 = answer(hidden_1, grads_1, *weights, 1, ())
    ring_0.step()
    back_1 = exchange(gate(ret_1, *ring_1.now()))
    ring_0.step()
    shard_0 = ring_0.finish()
    sums_0 = unpack(pick[0], back_0, 0, ())
    ring_1.step()
    ring_1.step(sums_0)
    ring_1.step()
    shard_1 = ring_1.finish()
    layer_out, grad_tokens = unpack(pick[1], back_1, 1, sums_0)
    shards = jnp.stack([shard_0, shard_1])
    return (
        layer_out,
        grad_tokens,
        shards[:, :GATE_ROWS, :HID],
        shards[:, :GATE_ROWS, HID:],
        shards[:, GATE_ROWS:, :],
    )


def solution(mesh):
    return jax.shard_map(
        per_device,
        mesh=mesh,
        in_specs=(
            P(("dp", "expert"), None),
            P(("dp", "expert"), None),
            P(("dp", "expert")),
            P(("dp", "expert"), None),
            P("expert", None, None),
            P("expert", None, None),
            P("expert", None, None),
        ),
        out_specs=(
            P(("dp", "expert"), None),
            P(("dp", "expert"), None),
            P("expert", "dp", None),
            P("expert", "dp", None),
            P("expert", "dp", None),
        ),
        check_vma=False,
    )
```

time: 194 us -> 179 us (0.923)
  blocking collectives: 39.1 us -> 0 us
  Pallas kernels: 30.5 us -> 42.1 us
  waiting for transfers between devices: 60.3 us -> 71.6 us
  starting transfers between devices: 42.5 us -> 48.6 us
  local copies, waits for them, and re-layouts: 5.05 us -> 2.27 us
  other arithmetic: 14.6 us -> 12.4 us
    all_to_all x1 -> x0, blocking collectives: 39.1 us -> none  [per_device(): recv = lax.all_to_all(send, 'expert', 0, 0, tiled=True)]
    pallas_call x4 -> x11, Pallas kernels: 30.5 us -> 42.1 us  [the longest x2 15.6 us: expert(): pl.pallas_call(functools.partial(expert_kernel, chunk, len(after)), out_s...]
    all_to_all x3 -> x4, starting transfers between devices: 16.6 us -> 25.2 us  [exchange(): return lax.all_to_all(rows, 'expert', 0, 0, tiled=True)]
    ppermute x16, waiting for transfers between devices: 38.7 us -> 44.5 us  [ring_step(): return lax.ppermute(held, 'dp', step)]
    all_to_all x3 -> x4, waiting for transfers between devices: 21.5 us -> 27.1 us  [exchange(): return lax.all_to_all(rows, 'expert', 0, 0, tiled=True)]
    unnamed x34 -> x18, local copies, waits for them, and re-layouts: 4.99 us -> 2.21 us
    ppermute x16, starting transfers between devices: 25.9 us -> 23.4 us  [ring_step(): return lax.ppermute(held, 'dp', step)]
    convert_element_type x10, other arithmetic: 10.3 us -> 8.06 us  [add_part(): return (held.astype(F32) + part.astype(F32)).astype(BF16)]
  transfers between devices with their start and end apart: 19 -> 20, of which waited for: 10 -> 12; matrix products, arithmetic and copies ran while one was open for 8% -> 7% of each run, Pallas kernels for 12% -> 19%
where the time goes in v2:
time: 179 us; the launch traced here: 178 us
  waiting for transfers between devices  71.6 us (40%)
  starting transfers between devices  48.6 us (27%)
  Pallas kernels  42.1 us (24%)
  other arithmetic  12.4 us (7%)
  local copies, waits for them, and re-layouts  2.27 us (1%)
    ppermute x16, waiting for transfers between devices, ring_step(): return lax.ppermute(held, 'dp', step)  44.5 us
    all_to_all x4, waiting for transfers between devices, exchange(): return lax.all_to_all(rows, 'expert', 0, 0, tiled=True)  27.1 us
    all_to_all x4, starting transfers between devices, exchange(): return lax.all_to_all(rows, 'expert', 0, 0, tiled=True)  25.2 us
    ppermute x16, starting transfers between devices, ring_step(): return lax.ppermute(held, 'dp', step)  23.4 us
    pallas_call x2, Pallas kernels, expert(): pl.pallas_call(functools.partial(expert_kernel, chunk, len(after)), out_s...  15.6 us
    pallas_call x2, Pallas kernels, answer(): pl.pallas_call(answer_kernel, grid=(steps,), out_shape=pltpu.HBM((GROUPS,...  10.8 us
    pallas_call x2, Pallas kernels, pack(): pl.pallas_call(functools.partial(pack_kernel, chunk), grid=(steps,), out_...  8.06 us
    convert_element_type x10, other arithmetic, add_part(): return (held.astype(F32) + part.astype(F32)).astype(BF16)  8.06 us
  transfers between devices with their start and end apart: 20, of which 12 were waited for; matrix products, arithmetic and copies ran while one was open for 7% of the time, Pallas kernels for 19%

profile of v2, /device:TPU:1, one launch (start us, length us, event | category | flops | bytes accessed | tf_op | source)
XLA Modules:
  0.0 177.9 jit_solution(14403081815697261088)
XLA Ops:
  0.6 4.8 %pack_0.1 = bf16[16,2,40,1024]{3,2,1,0:T(8,128)(2,1)} custom-call(s32[2,256]{1,0:T(2,128)} %bitcast.19, s32[1,256]{1,0:T(1,128)} %bitcast.22, bf16[256,1024]{1,0:T(8,128)(2,1)} %tokens_ref.3, bf16[256,1024]{1,0:T(8,128)(2,1)} %cot_ref.3), custom_call_target="tpu_custom_call" | custom-call | flops 671088640 | bytes 4194304 | tf_op jit(solution)/shard_map/pack_0/pallas_call | solution.py:81
  5.4 7.6 %all-to-all-start.1 = ((bf16[16,2,40,1024]{3,2,1,0:T(8,128)(2,1)}), bf16[16,2,40,1024]{3,2,1,0:T(8,128)(2,1)}, u32[]{:S(2)}, u32[]{:S(2)}) async-start(bf16[16,2,40,1024]{3,2,1,0:T(8,128)(2,1)} %pack_0.1), calls=%async_computation.1 | async-start | bytes 5242880 | tf_op jit(solution)/shard_map/all_to_all | solution.py:327
  16.7 3.3 %pack_1.1 = bf16[16,2,40,1024]{3,2,1,0:T(8,128)(2,1)} custom-call(s32[2,256]{1,0:T(2,128)S(1)} %bitcast.21, s32[1,256]{1,0:T(1,128)S(1)} %bitcast.24, bf16[256,1024]{1,0:T(8,128)(2,1)S(1)} %copy-done.2, bf16[256,1024]{1,0:T(8,128)(2,1)S(1)} %copy-done.3, bf16[2,256,640]{2,1,0:T(8,128)(2,1)S(1)} %copy-done, bf16[2,256,640]{2,1,0:T(8,128)(2,1)S(1)} %copy-done.1), custom_call_target="tpu_custom_call" | custom-call | flops 671088640 | bytes 4194304 | tf_op jit(solution)/shard_map/pack_1/pallas_call | solution.py:81
  20.0 25.9 %all-to-all-done.1.recv_ref = bf16[16,2,40,1024]{3,2,1,0:T(8,128)(2,1)} async-done(((bf16[16,2,40,1024]{3,2,1,0:T(8,128)(2,1)}), bf16[16,2,40,1024]{3,2,1,0:T(8,128)(2,1)}, u32[]{:S(2)}, u32[]{:S(2)}) %all-to-all-start.1) | async-done | bytes 2621472 | tf_op jit(solution)/shard_map/all_to_all | solution.py:327
  45.9 5.1 %all-to-all-start = ((bf16[16,2,40,1024]{3,2,1,0:T(8,128)(2,1)}), bf16[16,2,40,1024]{3,2,1,0:T(8,128)(2,1)}, u32[]{:S(2)}, u32[]{:S(2)}) async-start(bf16[16,2,40,1024]{3,2,1,0:T(8,128)(2,1)} %pack_1.1), calls=%async_computation | async-start | bytes 5242880 | tf_op jit(solution)/shard_map/all_to_all | solution.py:327
  51.0 7.8 %expert_0.1 = (bf16[640,512]{1,0:T(8,128)(2,1)S(1)}, bf16[640,1024]{1,0:T(8,128)(2,1)S(1)}, bf16[2,96,1024]{2,1,0:T(8,128)(2,1)S(1)}, bf16[2,96,1024]{2,1,0:T(8,...) custom-call(s32[1]{0:T(128)} %bitcast.2.z_ref, ...), custom_call_target="tpu_custom_call" | custom-call | flops 4026531840 | bytes 10485760 | tf_op jit(solution)/shard_map/expert_0/pallas_call | solution.py:164
  59.9 4.0 %collective-permute-start.2 = (bf16[2,96,1024]{2,1,0:T(8,128)(2,1)S(1)}, bf16[2,96,1024]{2,1,0:T(8,128)(2,1)S(1)}, u32[]{:S(2)}, u32[]{:S(2)}) collective-permute-start(bf16[2,96,1024]{2,1,0:T(8,128)(2,1)S(1)} %get-tuple-element.37), channel_id=1, source_target_pairs={{0,224},{16,240},{32,0},{48,16},{64,32},{80,48},{96,64},{112,80},{... | collective-permute-start | bytes 1179656 | tf_op jit(solution)/shard_map/ppermute | solution.py:269
  63.9 9.3 %collective-permute-done = bf16[2,96,1024]{2,1,0:T(8,128)(2,1)S(1)} collective-permute-done((bf16[2,96,1024]{2,1,0:T(8,128)(2,1)S(1)}, bf16[2,96,1024]{2,1,0:T(8,128)(2,1)S(1)}, u32[]{:S(2)}, u32[]{:S(2)}) %collective-permute-start) | collective-permute-done | bytes 393248 | tf_op jit(solution)/shard_map/ppermute | solution.py:269
  73.6 2.7 %collective-permute-start.3 = (bf16[2,96,1024]{2,1,0:T(8,128)(2,1)S(1)}, bf16[2,96,1024]{2,1,0:T(8,128)(2,1)S(1)}, u32[]{:S(2)}, u32[]{:S(2)}) collective-permute-start(bf16[2,96,1024]{2,1,0:T(8,128)(2,1)S(1)} %add_convert_fusion.7.refs_2_), channel_id=1, source_target_pairs={{0,224},{16,240},{32,0},{48,16},{64,32},{80,48},{96,64},{112,80},{... | collective-permute-start | bytes 1179656 | tf_op jit(solution)/shard_map/ppermute | solution.py:269
  76.3 5.4 %answer_0.1.refs_0_ = bf16[16,2,40,1024]{3,2,1,0:T(8,128)(2,1)} custom-call(bf16[640,512]{1,0:T(8,128)(2,1)S(1)} %get-tuple-element.46.hidden_ref, bf16[640,1024]{1,0:T(8,128)(2,1)S(1)} %get-tuple-element.47.grads_ref, bf16[2,1024,512]{2,1,0:T(8,128)(2,1)} %gate_ref.7, bf16[2,1024,512]{2,1,0:T(8,128)(2,1)} %up_ref.7, bf16[2,512,1024]{2,1,0:T(8,128)(2,1)} %down_ref.7), custom_call_target="tpu_custom_call" | custom-call | flops 2013265920 | bytes 8388608 | tf_op jit(solution)/shard_map/answer_0/pallas_call | solution.py:197
  81.7 3.0 %collective-permute-done.1 = bf16[2,96,1024]{2,1,0:T(8,128)(2,1)} collective-permute-done((bf16[2,96,1024]{2,1,0:T(8,128)(2,1)S(1)}, bf16[2,96,1024]{2,1,0:T(8,128)(2,1)}, u32[]{:S(2)}, u32[]{:S(2)}) %collective-permute-start.1) | collective-permute-done | bytes 393248 | tf_op jit(solution)/shard_map/ppermute | solution.py:269
  85.8 6.9 %all-to-all-start.3 = ((bf16[16,2,40,1024]{3,2,1,0:T(8,128)(2,1)}), bf16[16,2,40,1024]{3,2,1,0:T(8,128)(2,1)}, u32[]{:S(2)}, u32[]{:S(2)}) async-start(bf16[16,2,40,1024]{3,2,1,0:T(8,128)(2,1)} %gate.3), calls=%async_computation.3 | async-start | bytes 5242880 | tf_op jit(solution)/shard_map/all_to_all | solution.py:327
  92.9 7.8 %expert_1.1 = (bf16[640,512]{1,0:T(8,128)(2,1)S(1)}, bf16[640,1024]{1,0:T(8,128)(2,1)S(1)}, bf16[2,96,1024]{2,1,0:T(8,128)(2,1)S(1)}, bf16[2,96,1024]{2,1,0:T(8,...) custom-call(s32[1]{0:T(128)} %bitcast.2.z_ref, ...), custom_call_target="tpu_custom_call" | custom-call | flops 12079595520 | bytes 31457280 | tf_op jit(solution)/shard_map/expert_1/pallas_call | solution.py:164
  104.9 7.7 %collective-permute-done.4 = bf16[2,96,1024]{2,1,0:T(8,128)(2,1)S(1)} collective-permute-done((bf16[2,96,1024]{2,1,0:T(8,128)(2,1)S(1)}, bf16[2,96,1024]{2,1,0:T(8,128)(2,1)S(1)}, u32[]{:S(2)}, u32[]{:S(2)}) %collective-permute-start.4) | collective-permute-done | bytes 393248 | tf_op jit(solution)/shard_map/ppermute | solution.py:269
  113.6 5.4 %answer_1.1.refs_0_ = bf16[16,2,40,1024]{3,2,1,0:T(8,128)(2,1)} custom-call(bf16[640,512]{1,0:T(8,128)(2,1)S(1)} %get-tuple-element.40.hidden_ref, bf16[640,1024]{1,0:T(8,128)(2,1)S(1)} %get-tuple-element.41.grads_ref, bf16[2,1024,512]{2,1,0:T(8,128)(2,1)} %gate_ref.7, bf16[2,1024,512]{2,1,0:T(8,128)(2,1)} %up_ref.7, bf16[2,512,1024]{2,1,0:T(8,128)(2,1)} %down_ref.7), custom_call_target="tpu_custom_call" | custom-call | flops 2013265920 | bytes 8388608 | tf_op jit(solution)/shard_map/answer_1/pallas_call | solution.py:197
  121.0 3.4 %collective-permute-start.13 = (bf16[2,96,1024]{2,1,0:T(8,128)(2,1)}, bf16[2,96,1024]{2,1,0:T(8,128)(2,1)S(1)}, u32[]{:S(2)}, u32[]{:S(2)}) collective-permute-start(bf16[2,96,1024]{2,1,0:T(8,128)(2,1)} %add_convert_fusion.4.refs_2_), channel_id=1, source_target_pairs={{0,224},{16,240},{32,0},{48,16},{64,32},{80,48},{96,64},{112,80},{... | collective-permute-start | bytes 1179656 | tf_op jit(solution)/shard_map/ppermute | solution.py:269
  125.6 5.7 %all-to-all-start.2 = ((bf16[16,2,40,1024]{3,2,1,0:T(8,128)(2,1)}), bf16[16,2,40,1024]{3,2,1,0:T(8,128)(2,1)}, u32[]{:S(2)}, u32[]{:S(2)}) async-start(bf16[16,2,40,1024]{3,2,1,0:T(8,128)(2,1)} %gate.2), calls=%async_computation.2 | async-start | bytes 5242880 | tf_op jit(solution)/shard_map/all_to_all | solution.py:327
  137.9 2.8 %unpack_0.1 = (f32[256,1024]{1,0:T(8,128)S(1)}, f32[256,1024]{1,0:T(8,128)S(1)}) custom-call(bf16[2,256,640]{2,1,0:T(8,128)(2,1)} %get-tuple-element.33.refs_0_.pick_ref, bf16[16,2,40,1024]{3,2,1,0:T(8,128)(2,1)} %all-to-all-done.3.ret_ref), custom_call_target="tpu_custom_call" | custom-call | flops 671088640 | bytes 4194304 | tf_op jit(solution)/shard_map/unpack_0/pallas_call | solution.py:231
  140.7 3.6 %collective-permute-done.11 = bf16[2,96,1024]{2,1,0:T(8,128)(2,1)S(1)} collective-permute-done((bf16[2,96,1024]{2,1,0:T(8,128)(2,1)S(1)}, bf16[2,96,1024]{2,1,0:T(8,128)(2,1)S(1)}, u32[]{:S(2)}, u32[]{:S(2)}) %collective-permute-start.11) | collective-permute-done | bytes 393248 | tf_op jit(solution)/shard_map/ppermute | solution.py:269
  149.3 4.5 %collective-permute-done.14 = bf16[2,96,1024]{2,1,0:T(8,128)(2,1)} collective-permute-done((bf16[2,96,1024]{2,1,0:T(8,128)(2,1)}, bf16[2,96,1024]{2,1,0:T(8,128)(2,1)}, u32[]{:S(2)}, u32[]{:S(2)}) %collective-permute-start.14) | collective-permute-done | bytes 393248 | tf_op jit(solution)/shard_map/ppermute | solution.py:269
  153.8 2.7 %collective-permute-done.12 = bf16[2,96,1024]{2,1,0:T(8,128)(2,1)} collective-permute-done((bf16[2,96,1024]{2,1,0:T(8,128)(2,1)}, bf16[2,96,1024]{2,1,0:T(8,128)(2,1)}, u32[]{:S(2)}, u32[]{:S(2)}) %collective-permute-start.12) | collective-permute-done | bytes 393248 | tf_op jit(solution)/shard_map/ppermute | solution.py:269
  160.5 8.1 %collective-permute-done.9 = bf16[96,1024]{1,0:T(8,128)(2,1)S(1)} collective-permute-done((bf16[96,1024]{1,0:T(8,128)(2,1)S(1)}, bf16[96,1024]{1,0:T(8,128)(2,1)S(1)}, u32[]{:S(2)}, u32[]{:S(2)}) %collective-permute-start.9) | collective-permute-done | bytes 196640 | tf_op jit(solution)/shard_map/ppermute | solution.py:269
  168.7 4.2 %collective-permute-done.15 = bf16[96,1024]{1,0:T(8,128)(2,1)S(1)} collective-permute-done((bf16[96,1024]{1,0:T(8,128)(2,1)S(1)}, bf16[96,1024]{1,0:T(8,128)(2,1)S(1)}, u32[]{:S(2)}, u32[]{:S(2)}) %collective-permute-start.15) | collective-permute-done | bytes 196640 | tf_op jit(solution)/shard_map/ppermute | solution.py:269
  174.5 3.4 %unpack_1.1 = (bf16[256,1024]{1,0:T(8,128)(2,1)}, bf16[256,1024]{1,0:T(8,128)(2,1)}) custom-call(bf16[2,256,640]{2,1,0:T(8,128)(2,1)} %get-tuple-element.32.refs_1_.pick_ref, bf16[16,2,40,1024]{3,2,1,0:T(8,128)(2,1)} %all-to-all-done.2.ret_ref, f32[256,1024]{1,0:T(8,128)S(1)} %get-tuple-element.48.refs_0_, f32[256,1024]{1,0:T(8,128)S(1)} %get-tuple-element.49.refs_1_), custom_call_target="tpu_custom_call" | custom-call | flops 671088640 | bytes 4194304 | tf_op jit(solution)/shard_map/unpack_1/pallas_call | solution.py:231
  (63 shorter events, 32.0 us)
Async XLA Ops:
  5.4 9.2 %copy-start.2 = (bf16[256,1024]{1,0:T(8,128)(2,1)S(1)}, bf16[256,1024]{1,0:T(8,128)(2,1)}, u32[]{:S(2)}) copy-start(bf16[256,1024]{1,0:T(8,128)(2,1)} %tokens_ref.3) | copy-start | bytes 1572868
  5.4 9.2 %copy-start.3 = (bf16[256,1024]{1,0:T(8,128)(2,1)S(1)}, bf16[256,1024]{1,0:T(8,128)(2,1)}, u32[]{:S(2)}) copy-start(bf16[256,1024]{1,0:T(8,128)(2,1)} %cot_ref.3) | copy-start | bytes 1572868
  5.4 40.5 %all-to-all-start.1 = ((bf16[16,2,40,1024]{3,2,1,0:T(8,128)(2,1)}), bf16[16,2,40,1024]{3,2,1,0:T(8,128)(2,1)}, u32[]{:S(2)}, u32[]{:S(2)}) async-start(bf16[16,2,40,1024]{3,2,1,0:T(8,128)(2,1)} %pack_0.1), calls=%async_computation.1 | async-start | bytes 5242880 | tf_op jit(solution)/shard_map/all_to_all | solution.py:327
  45.9 39.9 %all-to-all-start = ((bf16[16,2,40,1024]{3,2,1,0:T(8,128)(2,1)}), bf16[16,2,40,1024]{3,2,1,0:T(8,128)(2,1)}, u32[]{:S(2)}, u32[]{:S(2)}) async-start(bf16[16,2,40,1024]{3,2,1,0:T(8,128)(2,1)} %pack_1.1), calls=%async_computation | async-start | bytes 5242880 | tf_op jit(solution)/shard_map/all_to_all | solution.py:327
  58.8 14.4 %collective-permute-start = (bf16[2,96,1024]{2,1,0:T(8,128)(2,1)S(1)}, bf16[2,96,1024]{2,1,0:T(8,128)(2,1)S(1)}, u32[]{:S(2)}, u32[]{:S(2)}) collective-permute-start(bf16[2,96,1024]{2,1,0:T(8,128)(2,1)S(1)} %get-tuple-element.34), channel_id=1, source_target_pairs={{0,32},{16,48},{32,64},{48,80},{64,96},{80,112},{96,128},{112,144}... | collective-permute-start | bytes 1179656 | tf_op jit(solution)/shard_map/ppermute | solution.py:269
  59.9 13.6 %collective-permute-start.2 = (bf16[2,96,1024]{2,1,0:T(8,128)(2,1)S(1)}, bf16[2,96,1024]{2,1,0:T(8,128)(2,1)S(1)}, u32[]{:S(2)}, u32[]{:S(2)}) collective-permute-start(bf16[2,96,1024]{2,1,0:T(8,128)(2,1)S(1)} %get-tuple-element.37), channel_id=1, source_target_pairs={{0,224},{16,240},{32,0},{48,16},{64,32},{80,48},{96,64},{112,80},{... | collective-permute-start | bytes 1179656 | tf_op jit(solution)/shard_map/ppermute | solution.py:269
  73.3 8.4 %copy-start.8 = (bf16[2,96,1024]{2,1,0:T(8,128)(2,1)}, bf16[2,96,1024]{2,1,0:T(8,128)(2,1)S(1)}, u32[]{:S(2)}) copy-start(bf16[2,96,1024]{2,1,0:T(8,128)(2,1)S(1)} %add_convert_fusion.9.refs_1_) | copy-start | bytes 1179652
  73.3 11.4 %collective-permute-start.1 = (bf16[2,96,1024]{2,1,0:T(8,128)(2,1)S(1)}, bf16[2,96,1024]{2,1,0:T(8,128)(2,1)}, u32[]{:S(2)}, u32[]{:S(2)}) collective-permute-start(bf16[2,96,1024]{2,1,0:T(8,128)(2,1)S(1)} %add_convert_fusion.9.refs_1_), channel_id=1, source_target_pairs={{0,32},{16,48},{32,64},{48,80},{64,96},{80,112},{96,128},{112,144}... | collective-permute-start | bytes 1179656 | tf_op jit(solution)/shard_map/ppermute | solution.py:269
  73.6 19.2 %collective-permute-start.3 = (bf16[2,96,1024]{2,1,0:T(8,128)(2,1)S(1)}, bf16[2,96,1024]{2,1,0:T(8,128)(2,1)S(1)}, u32[]{:S(2)}, u32[]{:S(2)}) collective-permute-start(bf16[2,96,1024]{2,1,0:T(8,128)(2,1)S(1)} %add_convert_fusion.7.refs_2_), channel_id=1, source_target_pairs={{0,224},{16,240},{32,0},{48,16},{64,32},{80,48},{96,64},{112,80},{... | collective-permute-start | bytes 1179656 | tf_op jit(solution)/shard_map/ppermute | solution.py:269
  85.8 39.7 %all-to-all-start.3 = ((bf16[16,2,40,1024]{3,2,1,0:T(8,128)(2,1)}), bf16[16,2,40,1024]{3,2,1,0:T(8,128)(2,1)}, u32[]{:S(2)}, u32[]{:S(2)}) async-start(bf16[16,2,40,1024]{3,2,1,0:T(8,128)(2,1)} %gate.3), calls=%async_computation.3 | async-start | bytes 5242880 | tf_op jit(solution)/shard_map/all_to_all | solution.py:327
  100.7 20.3 %copy-start.4 = (bf16[2,96,1024]{2,1,0:T(8,128)(2,1)}, bf16[2,96,1024]{2,1,0:T(8,128)(2,1)S(1)}, u32[]{:S(2)}) copy-start(bf16[2,96,1024]{2,1,0:T(8,128)(2,1)S(1)} %get-tuple-element.54) | copy-start | bytes 1179652
  100.7 12.0 %collective-permute-start.4 = (bf16[2,96,1024]{2,1,0:T(8,128)(2,1)S(1)}, bf16[2,96,1024]{2,1,0:T(8,128)(2,1)S(1)}, u32[]{:S(2)}, u32[]{:S(2)}) collective-permute-start(bf16[2,96,1024]{2,1,0:T(8,128)(2,1)S(1)} %get-tuple-element.42), channel_id=1, source_target_pairs={{0,32},{16,48},{32,64},{48,80},{64,96},{80,112},{96,128},{112,144}... | collective-permute-start | bytes 1179656 | tf_op jit(solution)/shard_map/ppermute | solution.py:269
  100.8 44.4 %collective-permute-start.6 = (bf16[2,96,1024]{2,1,0:T(8,128)(2,1)S(1)}, bf16[2,96,1024]{2,1,0:T(8,128)(2,1)}, u32[]{:S(2)}, u32[]{:S(2)}) collective-permute-start(bf16[2,96,1024]{2,1,0:T(8,128)(2,1)S(1)} %add_convert_fusion.8.refs_0_), channel_id=1, source_target_pairs={{0,32},{16,48},{32,64},{48,80},{64,96},{80,112},{96,128},{112,144}... | collective-permute-start | bytes 1179656 | tf_op jit(solution)/shard_map/ppermute | solution.py:269
  100.9 31.6 %collective-permute-start.7 = (bf16[2,96,1024]{2,1,0:T(8,128)(2,1)S(1)}, bf16[2,96,1024]{2,1,0:T(8,128)(2,1)}, u32[]{:S(2)}, u32[]{:S(2)}) collective-permute-start(bf16[2,96,1024]{2,1,0:T(8,128)(2,1)S(1)} %add_convert_fusion.6.refs_1_), channel_id=1, source_target_pairs={{0,224},{16,240},{32,0},{48,16},{64,32},{80,48},{96,64},{112,80},{... | collective-permute-start | bytes 1179656 | tf_op jit(solution)/shard_map/ppermute | solution.py:269
  103.6 16.5 %collective-permute-start.5 = (bf16[2,96,1024]{2,1,0:T(8,128)(2,1)S(1)}, bf16[2,96,1024]{2,1,0:T(8,128)(2,1)S(1)}, u32[]{:S(2)}, u32[]{:S(2)}) collective-permute-start(bf16[2,96,1024]{2,1,0:T(8,128)(2,1)S(1)} %get-tuple-element.44), channel_id=1, source_target_pairs={{0,224},{16,240},{32,0},{48,16},{64,32},{80,48},{96,64},{112,80},{... | collective-permute-start | bytes 1179656 | tf_op jit(solution)/shard_map/ppermute | solution.py:269
  113.6 17.7 %collective-permute-start.10 = (bf16[2,96,1024]{2,1,0:T(8,128)(2,1)}, bf16[2,96,1024]{2,1,0:T(8,128)(2,1)}, u32[]{:S(2)}, u32[]{:S(2)}) collective-permute-start(bf16[2,96,1024]{2,1,0:T(8,128)(2,1)} %add_convert_fusion.5.refs_1_), channel_id=1, source_target_pairs={{0,32},{16,48},{32,64},{48,80},{64,96},{80,112},{96,128},{112,144}... | collective-permute-start | bytes 1179656 | tf_op jit(solution)/shard_map/ppermute | solution.py:269
  121.0 16.1 %collective-permute-start.13 = (bf16[2,96,1024]{2,1,0:T(8,128)(2,1)}, bf16[2,96,1024]{2,1,0:T(8,128)(2,1)S(1)}, u32[]{:S(2)}, u32[]{:S(2)}) collective-permute-start(bf16[2,96,1024]{2,1,0:T(8,128)(2,1)} %add_convert_fusion.4.refs_2_), channel_id=1, source_target_pairs={{0,224},{16,240},{32,0},{48,16},{64,32},{80,48},{96,64},{112,80},{... | collective-permute-start | bytes 1179656 | tf_op jit(solution)/shard_map/ppermute | solution.py:269
  125.6 48.9 %all-to-all-start.2 = ((bf16[16,2,40,1024]{3,2,1,0:T(8,128)(2,1)}), bf16[16,2,40,1024]{3,2,1,0:T(8,128)(2,1)}, u32[]{:S(2)}, u32[]{:S(2)}) async-start(bf16[16,2,40,1024]{3,2,1,0:T(8,128)(2,1)} %gate.2), calls=%async_computation.2 | async-start | bytes 5242880 | tf_op jit(solution)/shard_map/all_to_all | solution.py:327
  132.4 12.0 %collective-permute-start.11 = (bf16[2,96,1024]{2,1,0:T(8,128)(2,1)S(1)}, bf16[2,96,1024]{2,1,0:T(8,128)(2,1)S(1)}, u32[]{:S(2)}, u32[]{:S(2)}) collective-permute-start(bf16[2,96,1024]{2,1,0:T(8,128)(2,1)S(1)} %add_convert_fusion.2), channel_id=1, source_target_pairs={{0,32},{16,48},{32,64},{48,80},{64,96},{80,112},{96,128},{112,144}... | collective-permute-start | bytes 1179656 | tf_op jit(solution)/shard_map/ppermute | solution.py:269
  134.4 11.0 %collective-permute-start.8 = (bf16[2,96,1024]{2,1,0:T(8,128)(2,1)}, bf16[2,96,1024]{2,1,0:T(8,128)(2,1)}, u32[]{:S(2)}, u32[]{:S(2)}) collective-permute-start(bf16[2,96,1024]{2,1,0:T(8,128)(2,1)} %add_convert_fusion.3), channel_id=1, source_target_pairs={{0,224},{16,240},{32,0},{48,16},{64,32},{80,48},{96,64},{112,80},{... | collective-permute-start | bytes 1179656 | tf_op jit(solution)/shard_map/ppermute | solution.py:269
  137.9 15.9 %collective-permute-start.14 = (bf16[2,96,1024]{2,1,0:T(8,128)(2,1)}, bf16[2,96,1024]{2,1,0:T(8,128)(2,1)}, u32[]{:S(2)}, u32[]{:S(2)}) collective-permute-start(bf16[2,96,1024]{2,1,0:T(8,128)(2,1)} %add_convert_fusion), channel_id=1, source_target_pairs={{0,224},{16,240},{32,0},{48,16},{64,32},{80,48},{96,64},{112,80},{... | collective-permute-start | bytes 1179656 | tf_op jit(solution)/shard_map/ppermute | solution.py:269
  145.2 11.3 %collective-permute-start.12 = (bf16[2,96,1024]{2,1,0:T(8,128)(2,1)}, bf16[2,96,1024]{2,1,0:T(8,128)(2,1)}, u32[]{:S(2)}, u32[]{:S(2)}) collective-permute-start(bf16[2,96,1024]{2,1,0:T(8,128)(2,1)} %add_convert_fusion.1), channel_id=1, source_target_pairs={{0,32},{16,48},{32,64},{48,80},{64,96},{80,112},{96,128},{112,144}... | collective-permute-start | bytes 1179656 | tf_op jit(solution)/shard_map/ppermute | solution.py:269
  146.7 21.9 %collective-permute-start.9 = (bf16[96,1024]{1,0:T(8,128)(2,1)S(1)}, bf16[96,1024]{1,0:T(8,128)(2,1)S(1)}, u32[]{:S(2)}, u32[]{:S(2)}) collective-permute-start(bf16[96,1024]{1,0:T(8,128)(2,1)S(1)} %fusion.4), channel_id=1, source_target_pairs={{0,16},{16,0},{32,48},{48,32},{64,80},{80,64},{96,112},{112,96},{1... | collective-permute-start | bytes 589832 | tf_op jit(solution)/shard_map/ppermute | solution.py:269
  158.0 14.9 %collective-permute-start.15 = (bf16[96,1024]{1,0:T(8,128)(2,1)S(1)}, bf16[96,1024]{1,0:T(8,128)(2,1)S(1)}, u32[]{:S(2)}, u32[]{:S(2)}) collective-permute-start(bf16[96,1024]{1,0:T(8,128)(2,1)S(1)} %fusion.5), channel_id=1, source_target_pairs={{0,16},{16,0},{32,48},{48,32},{64,80},{80,64},{96,112},{112,96},{1... | collective-permute-start | bytes 589832 | tf_op jit(solution)/shard_map/ppermute | solution.py:269
  (5 other events, 25.5 us)

commit v3 on v2

--- a/solution.py
+++ b/solution.py
@@ -183,7 +183,8 @@
 
 
 def answer_kernel(hidden_ref, grads_ref, gate_ref, up_ref, down_ref, *refs):
-    ret_ref = refs[-1]
+    ret_ref, token_ref = refs[-2:]
+    token_ref[...] = jnp.zeros_like(token_ref)
     groups = ret_ref.shape[0]
     out = mm(hidden_ref[...], down_ref[0])
     ret_ref[:, 0] = out.reshape(groups, CAP, D).astype(BF16)
@@ -197,14 +198,17 @@
     return pl.pallas_call(
         answer_kernel,
         grid=(steps,),
-        out_shape=pltpu.HBM((GROUPS, 2, CAP, D), BF16),
+        out_shape=[pltpu.HBM((GROUPS, 2, CAP, D), BF16), jax.ShapeDtypeStruct((8, 128), F32)],
         in_specs=[
             pl.BlockSpec((ROWS // steps, HID), lambda i: (i, 0)),
             pl.BlockSpec((ROWS // steps, 2 * HID), lambda i: (i, 0)),
         ]
         + [one(chunk, D, HID), one(chunk, D, HID), one(chunk, HID, D)]
         + [ANY] * len(after),
-        out_specs=pl.BlockSpec((GROUPS // steps, 2, CAP, D), lambda i: (i, 0, 0, 0)),
+        out_specs=[
+            pl.BlockSpec((GROUPS // steps, 2, CAP, D), lambda i: (i, 0, 0, 0)),
+            whole(8, 128),
+        ],
         compiler_params=pltpu.CompilerParams(vmem_limit_bytes=24 << 20),
         cost_estimate=pl.CostEstimate(
             flops=6 * ROWS * D * HID, bytes_accessed=8 << 20, transcendentals=0
@@ -336,14 +340,14 @@
     recv_1 = exchange(pack(ids, quant, tokens, cotangent, 1, pick))
     hidden_0, grads_0, parts_0 = expert(z, recv_0, *weights, 0, ())
     ring_0 = Ring(parts_0, 3)
-    ret_0 = answer(hidden_0, grads_0, *weights, 0, ())
+    ret_0, _ = answer(hidden_0, grads_0, *weights, 0, ())
     ring_0.step()
     back_0 = exchange(gate(ret_0, *ring_0.now()))
     ring_0.step()
     hidden_1, grads_1, parts_1 = expert(z, recv_1, *weights, 1, ring_0.now())
     ring_1 = Ring(parts_1, 4)
-    ring_1.step()
-    ret_1 = answer(hidden_1, grads_1, *weights, 1, ())
+    ret_1, token = answer(hidden_1, grads_1, *weights, 1, ())
+    ring_1.step((token,), (token,))
     ring_0.step()
     back_1 = exchange(gate(ret_1, *ring_1.now()))
     ring_0.step()

time: 179 us -> 173 us (0.966)
  waiting for transfers between devices: 71.6 us -> 63.7 us
  starting transfers between devices: 48.6 us -> 51.5 us
    ppermute x16, waiting for transfers between devices: 44.5 us -> 31.9 us  [ring_step(): return lax.ppermute(held, 'dp', step)]
    ppermute x16, starting transfers between devices: 23.4 us -> 28.7 us  [ring_step(): return lax.ppermute(held, 'dp', step)]
    all_to_all x4, waiting for transfers between devices: 27.1 us -> 31.8 us  [exchange(): return lax.all_to_all(rows, 'expert', 0, 0, tiled=True)]
    all_to_all x4, starting transfers between devices: 25.2 us -> 22.8 us  [exchange(): return lax.all_to_all(rows, 'expert', 0, 0, tiled=True)]
  transfers between devices with their start and end apart: 20 -> 20, of which waited for: 12 -> 11; matrix products, arithmetic and copies ran while one was open for 7% -> 7% of each run, Pallas kernels for 19% -> 20%
where the time goes in v3:
time: 173 us
  waiting for transfers between devices  63.7 us (37%)
  starting transfers between devices  51.5 us (30%)
  Pallas kernels  42.1 us (24%)
  other arithmetic  12.4 us (7%)
  local copies, waits for them, and re-layouts  2.27 us (1%)
    ppermute x16, waiting for transfers between devices, ring_step(): return lax.ppermute(held, 'dp', step)  31.9 us
    all_to_all x4, waiting for transfers between devices, exchange(): return lax.all_to_all(rows, 'expert', 0, 0, tiled=True)  31.8 us
    ppermute x16, starting transfers between devices, ring_step(): return lax.ppermute(held, 'dp', step)  28.7 us
    all_to_all x4, starting transfers between devices, exchange(): return lax.all_to_all(rows, 'expert', 0, 0, tiled=True)  22.8 us
    pallas_call x2, Pallas kernels, expert(): pl.pallas_call(functools.partial(expert_kernel, chunk, len(after)), out_s...  15.6 us
    pallas_call x2, Pallas kernels, answer(): pl.pallas_call(answer_kernel, grid=(steps,), out_shape=[pltpu.HBM((GROUPS...  10.8 us
    convert_element_type x10, other arithmetic, add_part(): return (held.astype(F32) + part.astype(F32)).astype(BF16)  8.07 us
    pallas_call x2, Pallas kernels, pack(): pl.pallas_call(functools.partial(pack_kernel, chunk), grid=(steps,), out_...  8.07 us
  transfers between devices with their start and end apart: 20, of which 11 were waited for; matrix products, arithmetic and copies ran while one was open for 7% of the time, Pallas kernels for 20%

profile of v3, /device:TPU:1, one launch (start us, length us, event | category | flops | bytes accessed | tf_op | source)
XLA Modules:
  0.0 172.8 jit_solution(12310591078015139263)
XLA Ops:
  0.6 4.8 %pack_0.1 = bf16[16,2,40,1024]{3,2,1,0:T(8,128)(2,1)} custom-call(s32[2,256]{1,0:T(2,128)} %bitcast.19, s32[1,256]{1,0:T(1,128)} %bitcast.22, bf16[256,1024]{1,0:T(8,128)(2,1)} %tokens_ref.3, bf16[256,1024]{1,0:T(8,128)(2,1)} %cot_ref.3), custom_call_target="tpu_custom_call" | custom-call | flops 671088640 | bytes 4194304 | tf_op jit(solution)/shard_map/pack_0/pallas_call | solution.py:81
  5.4 7.6 %all-to-all-start.1 = ((bf16[16,2,40,1024]{3,2,1,0:T(8,128)(2,1)}), bf16[16,2,40,1024]{3,2,1,0:T(8,128)(2,1)}, u32[]{:S(2)}, u32[]{:S(2)}) async-start(bf16[16,2,40,1024]{3,2,1,0:T(8,128)(2,1)} %pack_0.1), calls=%async_computation.1 | async-start | bytes 5242880 | tf_op jit(solution)/shard_map/all_to_all | solution.py:331
  16.7 3.3 %pack_1.1 = bf16[16,2,40,1024]{3,2,1,0:T(8,128)(2,1)} custom-call(s32[2,256]{1,0:T(2,128)S(1)} %bitcast.21, s32[1,256]{1,0:T(1,128)S(1)} %bitcast.24, bf16[256,1024]{1,0:T(8,128)(2,1)S(1)} %copy-done.2, bf16[256,1024]{1,0:T(8,128)(2,1)S(1)} %copy-done.3, bf16[2,256,640]{2,1,0:T(8,128)(2,1)S(1)} %copy-done, bf16[2,256,640]{2,1,0:T(8,128)(2,1)S(1)} %copy-done.1), custom_call_target="tpu_custom_call" | custom-call | flops 671088640 | bytes 4194304 | tf_op jit(solution)/shard_map/pack_1/pallas_call | solution.py:81
  20.0 25.9 %all-to-all-done.1.recv_ref = bf16[16,2,40,1024]{3,2,1,0:T(8,128)(2,1)} async-done(((bf16[16,2,40,1024]{3,2,1,0:T(8,128)(2,1)}), bf16[16,2,40,1024]{3,2,1,0:T(8,128)(2,1)}, u32[]{:S(2)}, u32[]{:S(2)}) %all-to-all-start.1) | async-done | bytes 2621472 | tf_op jit(solution)/shard_map/all_to_all | solution.py:331
  45.9 5.1 %all-to-all-start = ((bf16[16,2,40,1024]{3,2,1,0:T(8,128)(2,1)}), bf16[16,2,40,1024]{3,2,1,0:T(8,128)(2,1)}, u32[]{:S(2)}, u32[]{:S(2)}) async-start(bf16[16,2,40,1024]{3,2,1,0:T(8,128)(2,1)} %pack_1.1), calls=%async_computation | async-start | bytes 5242880 | tf_op jit(solution)/shard_map/all_to_all | solution.py:331
  51.0 7.8 %expert_0.1 = (bf16[640,512]{1,0:T(8,128)(2,1)S(1)}, bf16[640,1024]{1,0:T(8,128)(2,1)S(1)}, bf16[2,96,1024]{2,1,0:T(8,128)(2,1)S(1)}, bf16[2,96,1024]{2,1,0:T(8,...) custom-call(s32[1]{0:T(128)} %bitcast.2.z_ref, ...), custom_call_target="tpu_custom_call" | custom-call | flops 4026531840 | bytes 10485760 | tf_op jit(solution)/shard_map/expert_0/pallas_call | solution.py:164
  59.9 4.0 %collective-permute-start.2 = (bf16[2,96,1024]{2,1,0:T(8,128)(2,1)S(1)}, bf16[2,96,1024]{2,1,0:T(8,128)(2,1)S(1)}, u32[]{:S(2)}, u32[]{:S(2)}) collective-permute-start(bf16[2,96,1024]{2,1,0:T(8,128)(2,1)S(1)} %get-tuple-element.42), channel_id=1, source_target_pairs={{0,224},{16,240},{32,0},{48,16},{64,32},{80,48},{96,64},{112,80},{... | collective-permute-start | bytes 1179656 | tf_op jit(solution)/shard_map/ppermute | solution.py:273
  63.9 9.3 %collective-permute-done = bf16[2,96,1024]{2,1,0:T(8,128)(2,1)S(1)} collective-permute-done((bf16[2,96,1024]{2,1,0:T(8,128)(2,1)S(1)}, bf16[2,96,1024]{2,1,0:T(8,128)(2,1)S(1)}, u32[]{:S(2)}, u32[]{:S(2)}) %collective-permute-start) | collective-permute-done | bytes 393248 | tf_op jit(solution)/shard_map/ppermute | solution.py:273
  73.6 2.7 %collective-permute-start.3 = (bf16[2,96,1024]{2,1,0:T(8,128)(2,1)S(1)}, bf16[2,96,1024]{2,1,0:T(8,128)(2,1)}, u32[]{:S(2)}, u32[]{:S(2)}) collective-permute-start(bf16[2,96,1024]{2,1,0:T(8,128)(2,1)S(1)} %add_convert_fusion.7.refs_2_), channel_id=1, source_target_pairs={{0,224},{16,240},{32,0},{48,16},{64,32},{80,48},{96,64},{112,80},{... | collective-permute-start | bytes 1179656 | tf_op jit(solution)/shard_map/ppermute | solution.py:273
  76.3 5.4 %answer_0.1 = (bf16[16,2,40,1024]{3,2,1,0:T(8,128)(2,1)}, f32[8,128]{1,0:T(8,128)}) custom-call(bf16[640,512]{1,0:T(8,128)(2,1)S(1)} %get-tuple-element.55.hidden_ref, bf16[640,1024]{1,0:T(8,128)(2,1)S(1)} %get-tuple-element.56.grads_ref, bf16[2,1024,512]{2,1,0:T(8,128)(2,1)} %gate_ref.7, bf16[2,1024,512]{2,1,0:T(8,128)(2,1)} %up_ref.7, ...), custom_call_target="tpu_custom_call" | custom-call | flops 2013265920 | bytes 8388608 | tf_op jit(solution)/shard_map/answer_0/pallas_call | solution.py:198
  83.9 5.1 %all-to-all-start.3 = ((bf16[16,2,40,1024]{3,2,1,0:T(8,128)(2,1)}), bf16[16,2,40,1024]{3,2,1,0:T(8,128)(2,1)}, u32[]{:S(2)}, u32[]{:S(2)}) async-start(bf16[16,2,40,1024]{3,2,1,0:T(8,128)(2,1)} %gate.3), calls=%async_computation.3 | async-start | bytes 5242880 | tf_op jit(solution)/shard_map/all_to_all | solution.py:331
  90.3 7.8 %expert_1.1 = (bf16[640,512]{1,0:T(8,128)(2,1)S(1)}, bf16[640,1024]{1,0:T(8,128)(2,1)S(1)}, bf16[2,96,1024]{2,1,0:T(8,128)(2,1)S(1)}, bf16[2,96,1024]{2,1,0:T(8,...) custom-call(s32[1]{0:T(128)} %bitcast.2.z_ref, ...), custom_call_target="tpu_custom_call" | custom-call | flops 12079595520 | bytes 31457280 | tf_op jit(solution)/shard_map/expert_1/pallas_call | solution.py:164
  99.1 4.0 %collective-permute-start.5 = (bf16[2,96,1024]{2,1,0:T(8,128)(2,1)S(1)}, bf16[2,96,1024]{2,1,0:T(8,128)(2,1)S(1)}, u32[]{:S(2)}, u32[]{:S(2)}) collective-permute-start(bf16[2,96,1024]{2,1,0:T(8,128)(2,1)S(1)} %get-tuple-element.52), channel_id=1, source_target_pairs={{0,224},{16,240},{32,0},{48,16},{64,32},{80,48},{96,64},{112,80},{... | collective-permute-start | bytes 1179656 | tf_op jit(solution)/shard_map/ppermute | solution.py:273
  103.2 5.4 %answer_1.1 = (bf16[16,2,40,1024]{3,2,1,0:T(8,128)(2,1)}, f32[8,128]{1,0:T(8,128)}) custom-call(bf16[640,512]{1,0:T(8,128)(2,1)S(1)} %get-tuple-element.45.hidden_ref, bf16[640,1024]{1,0:T(8,128)(2,1)S(1)} %get-tuple-element.46.grads_ref, bf16[2,1024,512]{2,1,0:T(8,128)(2,1)} %gate_ref.7, bf16[2,1024,512]{2,1,0:T(8,128)(2,1)} %up_ref.7, ...), custom_call_target="tpu_custom_call" | custom-call | flops 2013265920 | bytes 8388608 | tf_op jit(solution)/shard_map/answer_1/pallas_call | solution.py:198
  108.5 3.7 %collective-permute-done.4 = bf16[2,96,1024]{2,1,0:T(8,128)(2,1)S(1)} collective-permute-done((bf16[2,96,1024]{2,1,0:T(8,128)(2,1)S(1)}, bf16[2,96,1024]{2,1,0:T(8,128)(2,1)S(1)}, u32[]{:S(2)}, u32[]{:S(2)}) %collective-permute-start.4) | collective-permute-done | bytes 393248 | tf_op jit(solution)/shard_map/ppermute | solution.py:273
  118.2 3.7 %all-to-all-done.3.ret_ref = bf16[16,2,40,1024]{3,2,1,0:T(8,128)(2,1)} async-done(((bf16[16,2,40,1024]{3,2,1,0:T(8,128)(2,1)}), bf16[16,2,40,1024]{3,2,1,0:T(8,128)(2,1)}, u32[]{:S(2)}, u32[]{:S(2)}) %all-to-all-start.3) | async-done | bytes 2621472 | tf_op jit(solution)/shard_map/all_to_all | solution.py:331
  121.9 5.1 %all-to-all-start.2 = ((bf16[16,2,40,1024]{3,2,1,0:T(8,128)(2,1)}), bf16[16,2,40,1024]{3,2,1,0:T(8,128)(2,1)}, u32[]{:S(2)}, u32[]{:S(2)}) async-start(bf16[16,2,40,1024]{3,2,1,0:T(8,128)(2,1)} %gate.2), calls=%async_computation.2 | async-start | bytes 5242880 | tf_op jit(solution)/shard_map/all_to_all | solution.py:331
  131.1 4.0 %collective-permute-start.8 = (bf16[2,96,1024]{2,1,0:T(8,128)(2,1)}, bf16[2,96,1024]{2,1,0:T(8,128)(2,1)}, u32[]{:S(2)}, u32[]{:S(2)}) collective-permute-start(bf16[2,96,1024]{2,1,0:T(8,128)(2,1)} %add_convert_fusion.3), channel_id=1, source_target_pairs={{0,224},{16,240},{32,0},{48,16},{64,32},{80,48},{96,64},{112,80},{... | collective-permute-start | bytes 1179656 | tf_op jit(solution)/shard_map/ppermute | solution.py:273
  137.4 2.8 %unpack_0.1 = (f32[256,1024]{1,0:T(8,128)S(1)}, f32[256,1024]{1,0:T(8,128)S(1)}) custom-call(bf16[2,256,640]{2,1,0:T(8,128)(2,1)} %get-tuple-element.38.refs_0_.pick_ref, bf16[16,2,40,1024]{3,2,1,0:T(8,128)(2,1)} %all-to-all-done.3.ret_ref), custom_call_target="tpu_custom_call" | custom-call | flops 671088640 | bytes 4194304 | tf_op jit(solution)/shard_map/unpack_0/pallas_call | solution.py:235
  147.5 4.5 %collective-permute-done.14 = bf16[2,96,1024]{2,1,0:T(8,128)(2,1)} collective-permute-done((bf16[2,96,1024]{2,1,0:T(8,128)(2,1)}, bf16[2,96,1024]{2,1,0:T(8,128)(2,1)}, u32[]{:S(2)}, u32[]{:S(2)}) %collective-permute-start.14) | collective-permute-done | bytes 393248 | tf_op jit(solution)/shard_map/ppermute | solution.py:273
  152.0 2.9 %collective-permute-done.12 = bf16[2,96,1024]{2,1,0:T(8,128)(2,1)} collective-permute-done((bf16[2,96,1024]{2,1,0:T(8,128)(2,1)}, bf16[2,96,1024]{2,1,0:T(8,128)(2,1)}, u32[]{:S(2)}, u32[]{:S(2)}) %collective-permute-start.12) | collective-permute-done | bytes 393248 | tf_op jit(solution)/shard_map/ppermute | solution.py:273
  158.9 4.7 %collective-permute-done.9 = bf16[96,1024]{1,0:T(8,128)(2,1)S(1)} collective-permute-done((bf16[96,1024]{1,0:T(8,128)(2,1)S(1)}, bf16[96,1024]{1,0:T(8,128)(2,1)S(1)}, u32[]{:S(2)}, u32[]{:S(2)}) %collective-permute-start.9) | collective-permute-done | bytes 196640 | tf_op jit(solution)/shard_map/ppermute | solution.py:273
  163.7 4.2 %collective-permute-done.15 = bf16[96,1024]{1,0:T(8,128)(2,1)S(1)} collective-permute-done((bf16[96,1024]{1,0:T(8,128)(2,1)S(1)}, bf16[96,1024]{1,0:T(8,128)(2,1)S(1)}, u32[]{:S(2)}, u32[]{:S(2)}) %collective-permute-start.15) | collective-permute-done | bytes 196640 | tf_op jit(solution)/shard_map/ppermute | solution.py:273
  169.4 3.4 %unpack_1.1 = (bf16[256,1024]{1,0:T(8,128)(2,1)}, bf16[256,1024]{1,0:T(8,128)(2,1)}) custom-call(bf16[2,256,640]{2,1,0:T(8,128)(2,1)} %get-tuple-element.37.refs_1_.pick_ref, bf16[16,2,40,1024]{3,2,1,0:T(8,128)(2,1)} %all-to-all-done.2.ret_ref, f32[256,1024]{1,0:T(8,128)S(1)} %get-tuple-element.58.refs_0_, f32[256,1024]{1,0:T(8,128)S(1)} %get-tuple-element.59.refs_1_), custom_call_target="tpu_custom_call" | custom-call | flops 671088640 | bytes 4194304 | tf_op jit(solution)/shard_map/unpack_1/pallas_call | solution.py:235
  (63 shorter events, 35.0 us)
Async XLA Ops:
  5.4 9.2 %copy-start.2 = (bf16[256,1024]{1,0:T(8,128)(2,1)S(1)}, bf16[256,1024]{1,0:T(8,128)(2,1)}, u32[]{:S(2)}) copy-start(bf16[256,1024]{1,0:T(8,128)(2,1)} %tokens_ref.3) | copy-start | bytes 1572868
  5.4 9.2 %copy-start.3 = (bf16[256,1024]{1,0:T(8,128)(2,1)S(1)}, bf16[256,1024]{1,0:T(8,128)(2,1)}, u32[]{:S(2)}) copy-start(bf16[256,1024]{1,0:T(8,128)(2,1)} %cot_ref.3) | copy-start | bytes 1572868
  5.4 40.5 %all-to-all-start.1 = ((bf16[16,2,40,1024]{3,2,1,0:T(8,128)(2,1)}), bf16[16,2,40,1024]{3,2,1,0:T(8,128)(2,1)}, u32[]{:S(2)}, u32[]{:S(2)}) async-start(bf16[16,2,40,1024]{3,2,1,0:T(8,128)(2,1)} %pack_0.1), calls=%async_computation.1 | async-start | bytes 5242880 | tf_op jit(solution)/shard_map/all_to_all | solution.py:331
  45.9 38.0 %all-to-all-start = ((bf16[16,2,40,1024]{3,2,1,0:T(8,128)(2,1)}), bf16[16,2,40,1024]{3,2,1,0:T(8,128)(2,1)}, u32[]{:S(2)}, u32[]{:S(2)}) async-start(bf16[16,2,40,1024]{3,2,1,0:T(8,128)(2,1)} %pack_1.1), calls=%async_computation | async-start | bytes 5242880 | tf_op jit(solution)/shard_map/all_to_all | solution.py:331
  58.8 14.4 %collective-permute-start = (bf16[2,96,1024]{2,1,0:T(8,128)(2,1)S(1)}, bf16[2,96,1024]{2,1,0:T(8,128)(2,1)S(1)}, u32[]{:S(2)}, u32[]{:S(2)}) collective-permute-start(bf16[2,96,1024]{2,1,0:T(8,128)(2,1)S(1)} %get-tuple-element.39), channel_id=1, source_target_pairs={{0,32},{16,48},{32,64},{48,80},{64,96},{80,112},{96,128},{112,144}... | collective-permute-start | bytes 1179656 | tf_op jit(solution)/shard_map/ppermute | solution.py:273
  59.9 13.6 %collective-permute-start.2 = (bf16[2,96,1024]{2,1,0:T(8,128)(2,1)S(1)}, bf16[2,96,1024]{2,1,0:T(8,128)(2,1)S(1)}, u32[]{:S(2)}, u32[]{:S(2)}) collective-permute-start(bf16[2,96,1024]{2,1,0:T(8,128)(2,1)S(1)} %get-tuple-element.42), channel_id=1, source_target_pairs={{0,224},{16,240},{32,0},{48,16},{64,32},{80,48},{96,64},{112,80},{... | collective-permute-start | bytes 1179656 | tf_op jit(solution)/shard_map/ppermute | solution.py:273
  73.3 8.4 %copy-start.7 = (bf16[2,96,1024]{2,1,0:T(8,128)(2,1)}, bf16[2,96,1024]{2,1,0:T(8,128)(2,1)S(1)}, u32[]{:S(2)}) copy-start(bf16[2,96,1024]{2,1,0:T(8,128)(2,1)S(1)} %add_convert_fusion.9.refs_1_) | copy-start | bytes 1179652
  73.3 15.6 %collective-permute-start.1 = (bf16[2,96,1024]{2,1,0:T(8,128)(2,1)S(1)}, bf16[2,96,1024]{2,1,0:T(8,128)(2,1)S(1)}, u32[]{:S(2)}, u32[]{:S(2)}) collective-permute-start(bf16[2,96,1024]{2,1,0:T(8,128)(2,1)S(1)} %add_convert_fusion.9.refs_1_), channel_id=1, source_target_pairs={{0,32},{16,48},{32,64},{48,80},{64,96},{80,112},{96,128},{112,144}... | collective-permute-start | bytes 1179656 | tf_op jit(solution)/shard_map/ppermute | solution.py:273
  73.6 15.5 %collective-permute-start.3 = (bf16[2,96,1024]{2,1,0:T(8,128)(2,1)S(1)}, bf16[2,96,1024]{2,1,0:T(8,128)(2,1)}, u32[]{:S(2)}, u32[]{:S(2)}) collective-permute-start(bf16[2,96,1024]{2,1,0:T(8,128)(2,1)S(1)} %add_convert_fusion.7.refs_2_), channel_id=1, source_target_pairs={{0,224},{16,240},{32,0},{48,16},{64,32},{80,48},{96,64},{112,80},{... | collective-permute-start | bytes 1179656 | tf_op jit(solution)/shard_map/ppermute | solution.py:273
  83.9 38.0 %all-to-all-start.3 = ((bf16[16,2,40,1024]{3,2,1,0:T(8,128)(2,1)}), bf16[16,2,40,1024]{3,2,1,0:T(8,128)(2,1)}, u32[]{:S(2)}, u32[]{:S(2)}) async-start(bf16[16,2,40,1024]{3,2,1,0:T(8,128)(2,1)} %gate.3), calls=%async_computation.3 | async-start | bytes 5242880 | tf_op jit(solution)/shard_map/all_to_all | solution.py:331
  98.1 18.7 %copy-start.4 = (bf16[2,96,1024]{2,1,0:T(8,128)(2,1)}, bf16[2,96,1024]{2,1,0:T(8,128)(2,1)S(1)}, u32[]{:S(2)}) copy-start(bf16[2,96,1024]{2,1,0:T(8,128)(2,1)S(1)} %get-tuple-element.64) | copy-start | bytes 1179652
  98.1 14.2 %collective-permute-start.4 = (bf16[2,96,1024]{2,1,0:T(8,128)(2,1)S(1)}, bf16[2,96,1024]{2,1,0:T(8,128)(2,1)S(1)}, u32[]{:S(2)}, u32[]{:S(2)}) collective-permute-start(bf16[2,96,1024]{2,1,0:T(8,128)(2,1)S(1)} %get-tuple-element.48), channel_id=1, source_target_pairs={{0,32},{16,48},{32,64},{48,80},{64,96},{80,112},{96,128},{112,144}... | collective-permute-start | bytes 1179656 | tf_op jit(solution)/shard_map/ppermute | solution.py:273
  99.1 16.7 %collective-permute-start.5 = (bf16[2,96,1024]{2,1,0:T(8,128)(2,1)S(1)}, bf16[2,96,1024]{2,1,0:T(8,128)(2,1)S(1)}, u32[]{:S(2)}, u32[]{:S(2)}) collective-permute-start(bf16[2,96,1024]{2,1,0:T(8,128)(2,1)S(1)} %get-tuple-element.52), channel_id=1, source_target_pairs={{0,224},{16,240},{32,0},{48,16},{64,32},{80,48},{96,64},{112,80},{... | collective-permute-start | bytes 1179656 | tf_op jit(solution)/shard_map/ppermute | solution.py:273
  113.1 13.8 %collective-permute-start.10 = (bf16[2,96,1024]{2,1,0:T(8,128)(2,1)}, bf16[2,96,1024]{2,1,0:T(8,128)(2,1)}, u32[]{:S(2)}, u32[]{:S(2)}) collective-permute-start(bf16[2,96,1024]{2,1,0:T(8,128)(2,1)} %add_convert_fusion.5.refs_1_), channel_id=1, source_target_pairs={{0,32},{16,48},{32,64},{48,80},{64,96},{80,112},{96,128},{112,144}... | collective-permute-start | bytes 1179656 | tf_op jit(solution)/shard_map/ppermute | solution.py:273
  113.2 30.3 %collective-permute-start.6 = (bf16[2,96,1024]{2,1,0:T(8,128)(2,1)S(1)}, bf16[2,96,1024]{2,1,0:T(8,128)(2,1)}, u32[]{:S(2)}, u32[]{:S(2)}) collective-permute-start(bf16[2,96,1024]{2,1,0:T(8,128)(2,1)S(1)} %add_convert_fusion.8.refs_0_), channel_id=1, source_target_pairs={{0,32},{16,48},{32,64},{48,80},{64,96},{80,112},{96,128},{112,144}... | collective-permute-start | bytes 1179656 | tf_op jit(solution)/shard_map/ppermute | solution.py:273
  113.2 16.0 %collective-permute-start.7 = (bf16[2,96,1024]{2,1,0:T(8,128)(2,1)S(1)}, bf16[2,96,1024]{2,1,0:T(8,128)(2,1)}, u32[]{:S(2)}, u32[]{:S(2)}) collective-permute-start(bf16[2,96,1024]{2,1,0:T(8,128)(2,1)S(1)} %add_convert_fusion.6.refs_1_), channel_id=1, source_target_pairs={{0,224},{16,240},{32,0},{48,16},{64,32},{80,48},{96,64},{112,80},{... | collective-permute-start | bytes 1179656 | tf_op jit(solution)/shard_map/ppermute | solution.py:273
  116.8 18.3 %collective-permute-start.13 = (bf16[2,96,1024]{2,1,0:T(8,128)(2,1)}, bf16[2,96,1024]{2,1,0:T(8,128)(2,1)S(1)}, u32[]{:S(2)}, u32[]{:S(2)}) collective-permute-start(bf16[2,96,1024]{2,1,0:T(8,128)(2,1)} %add_convert_fusion.4.refs_2_), channel_id=1, source_target_pairs={{0,224},{16,240},{32,0},{48,16},{64,32},{80,48},{96,64},{112,80},{... | collective-permute-start | bytes 1179656 | tf_op jit(solution)/shard_map/ppermute | solution.py:273
  121.9 47.5 %all-to-all-start.2 = ((bf16[16,2,40,1024]{3,2,1,0:T(8,128)(2,1)}), bf16[16,2,40,1024]{3,2,1,0:T(8,128)(2,1)}, u32[]{:S(2)}, u32[]{:S(2)}) async-start(bf16[16,2,40,1024]{3,2,1,0:T(8,128)(2,1)} %gate.2), calls=%async_computation.2 | async-start | bytes 5242880 | tf_op jit(solution)/shard_map/all_to_all | solution.py:331
  128.1 14.4 %collective-permute-start.11 = (bf16[2,96,1024]{2,1,0:T(8,128)(2,1)S(1)}, bf16[2,96,1024]{2,1,0:T(8,128)(2,1)S(1)}, u32[]{:S(2)}, u32[]{:S(2)}) collective-permute-start(bf16[2,96,1024]{2,1,0:T(8,128)(2,1)S(1)} %add_convert_fusion.2), channel_id=1, source_target_pairs={{0,32},{16,48},{32,64},{48,80},{64,96},{80,112},{96,128},{112,144}... | collective-permute-start | bytes 1179656 | tf_op jit(solution)/shard_map/ppermute | solution.py:273
  131.1 12.5 %collective-permute-start.8 = (bf16[2,96,1024]{2,1,0:T(8,128)(2,1)}, bf16[2,96,1024]{2,1,0:T(8,128)(2,1)}, u32[]{:S(2)}, u32[]{:S(2)}) collective-permute-start(bf16[2,96,1024]{2,1,0:T(8,128)(2,1)} %add_convert_fusion.3), channel_id=1, source_target_pairs={{0,224},{16,240},{32,0},{48,16},{64,32},{80,48},{96,64},{112,80},{... | collective-permute-start | bytes 1179656 | tf_op jit(solution)/shard_map/ppermute | solution.py:273
  135.9 16.1 %collective-permute-start.14 = (bf16[2,96,1024]{2,1,0:T(8,128)(2,1)}, bf16[2,96,1024]{2,1,0:T(8,128)(2,1)}, u32[]{:S(2)}, u32[]{:S(2)}) collective-permute-start(bf16[2,96,1024]{2,1,0:T(8,128)(2,1)} %add_convert_fusion), channel_id=1, source_target_pairs={{0,224},{16,240},{32,0},{48,16},{64,32},{80,48},{96,64},{112,80},{... | collective-permute-start | bytes 1179656 | tf_op jit(solution)/shard_map/ppermute | solution.py:273
  143.4 11.5 %collective-permute-start.12 = (bf16[2,96,1024]{2,1,0:T(8,128)(2,1)}, bf16[2,96,1024]{2,1,0:T(8,128)(2,1)}, u32[]{:S(2)}, u32[]{:S(2)}) collective-permute-start(bf16[2,96,1024]{2,1,0:T(8,128)(2,1)} %add_convert_fusion.1), channel_id=1, source_target_pairs={{0,32},{16,48},{32,64},{48,80},{64,96},{80,112},{96,128},{112,144}... | collective-permute-start | bytes 1179656 | tf_op jit(solution)/shard_map/ppermute | solution.py:273
  144.9 18.7 %collective-permute-start.9 = (bf16[96,1024]{1,0:T(8,128)(2,1)S(1)}, bf16[96,1024]{1,0:T(8,128)(2,1)S(1)}, u32[]{:S(2)}, u32[]{:S(2)}) collective-permute-start(bf16[96,1024]{1,0:T(8,128)(2,1)S(1)} %fusion.4), channel_id=1, source_target_pairs={{0,16},{16,0},{32,48},{48,32},{64,80},{80,64},{96,112},{112,96},{1... | collective-permute-start | bytes 589832 | tf_op jit(solution)/shard_map/ppermute | solution.py:273
  156.4 11.4 %collective-permute-start.15 = (bf16[96,1024]{1,0:T(8,128)(2,1)S(1)}, bf16[96,1024]{1,0:T(8,128)(2,1)S(1)}, u32[]{:S(2)}, u32[]{:S(2)}) collective-permute-start(bf16[96,1024]{1,0:T(8,128)(2,1)S(1)} %fusion.5), channel_id=1, source_target_pairs={{0,16},{16,0},{32,48},{48,32},{64,80},{80,64},{96,112},{112,96},{1... | collective-permute-start | bytes 589832 | tf_op jit(solution)/shard_map/ppermute | solution.py:273
  (5 other events, 25.5 us)
